TPU v7x, 128 devices: a whole 4x4x4 slice. The times are simulated.
128 devices in a mesh: comp: 8 (over x, z_hi), band: 16 (over z_lo, y, core).
Axes of the slice: x: 4, y: 4, z: 4 (z_hi: 2, z_lo: 2; z = z_hi * 2 + z_lo), core: 2. Of those that a mesh axis runs over, the one named last changes fastest.
Arguments:
- estimate: float32 [1024, 256], P('band'), may hold values from -6 to 6
- residual: float32 [1024, 256], P('band'), may hold values from -50 to 50
- direction: float32 [1024, 256], P('band'), may hold values from -50 to 50
- kernels: bfloat16 [32, 65, 65], P('comp'), may hold values from -0.015625 to 0.015625
- weight_maps: bfloat16 [32, 1024, 256], P('comp', 'band'), may hold values from -6 to 6
- filters_in: float32 [64, 3, 3], replicated, may hold values from -2 to 2
- biases: float32 [64], replicated, may hold values from -3 to 3
- filters_out: float32 [64, 3, 3], replicated, may hold values from -0.25 to 0.25
Outputs:
- estimate_next: float32 [1024, 256], P('band')
- residual_next: float32 [1024, 256], P('band')
- direction_next: float32 [1024, 256], P('band')
- denoised: float32 [1024, 256], P('band', 'comp')
All inputs are finite; a program needn't handle non-finite values.
Results may differ from a plain program's by a relative error of at most 0.0024.
Values may be sent and summed in bfloat16 or wider, within the bound.
A program may use at most 64 MiB of HBM per device.

v0:
```python
import jax
import jax.numpy as jnp
from jax import lax
from jax.sharding import PartitionSpec as P

damping = 0.5


def with_halo(array, sides, width):
    for axis, dim in sides:
        count, length = (lax.axis_size(axis), array.shape[dim])
        up = [(i, (i + 1) % count) for i in range(count - 1)]
        down = [(j, i) for i, j in up]
        last = lax.slice_in_dim(array, length - width, length, axis=dim)
        first = lax.slice_in_dim(array, 0, width, axis=dim)
        before = lax.ppermute(last, axis, up)
        after = lax.ppermute(first, axis, down)
        array = jnp.concatenate([before, array, after], axis=dim)
    return array


def denoise(estimate_next, filters_in, biases, filters_out):
    rows, width = estimate_next.shape
    framed = with_halo(estimate_next, (("band", 0),), 2)
    columns = width // lax.axis_size("comp")
    start = lax.axis_index("comp") * columns
    padded = jnp.pad(framed, ((0, 0), (2, 2)))
    tile = lax.dynamic_slice_in_dim(padded, start, columns + 4, 1)
    taps = jnp.stack(
        [tile[a : a + rows + 2, b : b + columns + 2] for a in range(3) for b in range(3)]
    )
    channels = filters_in.shape[0]
    features = jnp.einsum(
        "ct,tij->cij", filters_in.reshape(channels, 9), taps, precision=lax.Precision.HIGHEST
    )
    features = jax.nn.relu(features + biases[:, None, None])
    total_rows = rows * lax.axis_size("band")
    global_rows = lax.axis_index("band") * rows - 1 + jnp.arange(rows + 2)
    global_cols = start - 1 + jnp.arange(columns + 2)
    inside_rows = (global_rows >= 0) & (global_rows < total_rows)
    inside_cols = (global_cols >= 0) & (global_cols < width)
    inside = (inside_rows[:, None] & inside_cols[None, :]).astype(jnp.float32)
    features = features * inside[None]
    spread = jnp.einsum(
        "ct,cij->tij", filters_out.reshape(channels, 9), features, precision=lax.Precision.HIGHEST
    )
    mixed = sum(
        (spread[a * 3 + b, a : a + rows, b : b + columns] for a in range(3) for b in range(3))
    )
    return tile[2 : 2 + rows, 2 : 2 + columns] - mixed


def correlate(source, taps):
    span = taps.shape[0]
    half = (span - 1) // 2
    source_rows, width = source.shape
    out_rows = source_rows - span + 1
    count = width // 128
    framed = jnp.pad(source, ((0, 0), (half, 128 - half)))
    lower = framed[:, :width].reshape(source_rows, count, 128)
    upper = framed[:, 128 : width + 128].reshape(source_rows, count, 128)
    blocks = jnp.concatenate([lower, upper], axis=2)
    offsets = jnp.arange(span)[:, None] + jnp.arange(out_rows)[None, :]
    stacked = blocks[offsets]
    spacing = jnp.arange(256)[:, None] - jnp.arange(128)[None, :]
    valid = (spacing >= 0) & (spacing < span)
    toeplitz = jnp.where(
        valid[None], taps[:, jnp.clip(spacing, 0, span - 1)], jnp.zeros((), taps.dtype)
    )
    result = jnp.einsum("arnu,auv->rnv", stacked, toeplitz, preferred_element_type=jnp.float32)
    return result.reshape(out_rows, width)


def blur_all(sources, kernels, out_rows, width):

    def add_one(total, pair):
        source, taps = pair
        return (total + correlate(source, taps), None)

    result, unused = lax.scan(
        add_one, jnp.zeros((out_rows, width), jnp.float32), (sources, kernels)
    )
    return result


def per_device(
    estimate, residual, direction, kernels, weight_maps, filters_in, biases, filters_out
):
    rows, width = direction.shape
    half = (kernels.shape[1] - 1) // 2
    maps_wide = weight_maps.astype(jnp.float32)
    shaped = (maps_wide * direction[None]).astype(jnp.bfloat16)
    padded = with_halo(shaped, (("band", 1),), half)
    partial_value = blur_all(padded, kernels, rows, width)
    image = lax.psum(partial_value, "comp").astype(jnp.bfloat16)
    edged = with_halo(image, (("band", 0),), half)
    flipped = kernels[:, ::-1, ::-1]

    def add_back(total, pair):
        taps, weights = pair
        return (total + weights * correlate(edged, taps), None)

    local_sum, unused = lax.scan(
        add_back, jnp.zeros((rows, width), jnp.float32), (flipped, maps_wide)
    )
    normal = lax.psum(local_sum, "comp")
    curved = normal + damping * direction
    old = lax.psum(jnp.sum(residual * residual), "band")
    product = lax.psum(jnp.sum(direction * curved), "band")
    alpha = old / product
    residual_next = residual - alpha * curved
    new = lax.psum(jnp.sum(residual_next * residual_next), "band")
    estimate_next = estimate + alpha * direction
    direction_next = residual_next + new / old * direction
    denoised = denoise(estimate_next, filters_in, biases, filters_out)
    return (estimate_next, residual_next, direction_next, denoised)


def solution(mesh):
    return jax.shard_map(
        per_device,
        mesh=mesh,
        in_specs=(
            P("band", None),
            P("band", None),
            P("band", None),
            P("comp", None, None),
            P("comp", "band", None),
            P(),
            P(),
            P(),
        ),
        out_specs=(P("band", None), P("band", None), P("band", None), P("band", "comp")),
        check_vma=False,
    )
```

profile of v0, /device:TPU:1, one launch (start us, length us, event | category | flops | bytes accessed | tf_op | source)
XLA Modules:
  0.0 1409.3 jit_solution(14927028550057009304)
XLA Ops:
  18.4 585.2 %while.26 = (s32[]{:T(128)}, f32[64,256]{1,0:T(8,128)S(1)}, bf16[4,128,256]{2,1,0:T(8,128)(2,1)S(1)}, bf16[4,65,65]{1,2,0:T(8,128)(2,1)S(1)}, s32[]{:T(128)}, /*index=5*/s32[]{:T(128)}) while((s32[]{:T(128)}, f32[64,256]{1,0:T(8,128)S(1)}, bf16[4,128,256]{2,1,0:T(8,128)(2,1)S(1)}, bf16[4,65,65]{1,2,0:T(8,128)(2,1)S(1)}, s32[]{:T(128)}, ...), condition=%wide.region_3.4_spmd.clone, body=%wide.region_2.3_spmd.clone.sunk | while | flops 548033792 | bytes 35641176 | solution.py:80
  18.9 16.3 %gather_fusion.1 = bf16[4160,2,256]{2,1,0:T(2,128)(2,1)} fusion(bf16[128,2,256]{2,1,0:T(2,128)(2,1)S(1)} %pad_maximum_fusion.6, s32[5120]{0:T(1024)S(1)} %pad_clamp_fusion.4), kind=kCustom, calls=%fused_computation.clone.clone.1 | custom fusion | bytes 8536320 | tf_op jit(solution)/shard_map/while/body/eval_jaxpr/gather | solution.py:64
  35.2 114.2 %gather_fusion = bf16[32768,65]{1,0:T(8,128)(2,1)} fusion(bf16[65,65]{0,1:T(8,128)(2,1)S(1)} %dynamic-slice_bitcast_fusion.6, s32[32768]{0:T(1024)S(1)} %fusion.73), kind=kCustom, calls=%fused_computation.1.clone.clone.1 | custom fusion | bytes 8650752 | tf_op jit(solution)/shard_map/while/body/eval_jaxpr/gather | solution.py:68
  165.2 16.3 %gather_fusion.1 = bf16[4160,2,256]{2,1,0:T(2,128)(2,1)} fusion(bf16[128,2,256]{2,1,0:T(2,128)(2,1)S(1)} %pad_maximum_fusion.6, s32[5120]{0:T(1024)S(1)} %pad_clamp_fusion.4), kind=kCustom, calls=%fused_computation.clone.clone.1 | custom fusion | bytes 8536320 | tf_op jit(solution)/shard_map/while/body/eval_jaxpr/gather | solution.py:64
  181.5 114.2 %gather_fusion = bf16[32768,65]{1,0:T(8,128)(2,1)} fusion(bf16[65,65]{0,1:T(8,128)(2,1)S(1)} %dynamic-slice_bitcast_fusion.6, s32[32768]{0:T(1024)S(1)} %fusion.73), kind=kCustom, calls=%fused_computation.1.clone.clone.1 | custom fusion | bytes 8650752 | tf_op jit(solution)/shard_map/while/body/eval_jaxpr/gather | solution.py:68
  311.5 16.3 %gather_fusion.1 = bf16[4160,2,256]{2,1,0:T(2,128)(2,1)} fusion(bf16[128,2,256]{2,1,0:T(2,128)(2,1)S(1)} %pad_maximum_fusion.6, s32[5120]{0:T(1024)S(1)} %pad_clamp_fusion.4), kind=kCustom, calls=%fused_computation.clone.clone.1 | custom fusion | bytes 8536320 | tf_op jit(solution)/shard_map/while/body/eval_jaxpr/gather | solution.py:64
  327.8 114.2 %gather_fusion = bf16[32768,65]{1,0:T(8,128)(2,1)} fusion(bf16[65,65]{0,1:T(8,128)(2,1)S(1)} %dynamic-slice_bitcast_fusion.6, s32[32768]{0:T(1024)S(1)} %fusion.73), kind=kCustom, calls=%fused_computation.1.clone.clone.1 | custom fusion | bytes 8650752 | tf_op jit(solution)/shard_map/while/body/eval_jaxpr/gather | solution.py:68
  457.8 16.3 %gather_fusion.1 = bf16[4160,2,256]{2,1,0:T(2,128)(2,1)} fusion(bf16[128,2,256]{2,1,0:T(2,128)(2,1)S(1)} %pad_maximum_fusion.6, s32[5120]{0:T(1024)S(1)} %pad_clamp_fusion.4), kind=kCustom, calls=%fused_computation.clone.clone.1 | custom fusion | bytes 8536320 | tf_op jit(solution)/shard_map/while/body/eval_jaxpr/gather | solution.py:64
  474.1 114.2 %gather_fusion = bf16[32768,65]{1,0:T(8,128)(2,1)} fusion(bf16[65,65]{0,1:T(8,128)(2,1)S(1)} %dynamic-slice_bitcast_fusion.6, s32[32768]{0:T(1024)S(1)} %fusion.73), kind=kCustom, calls=%fused_computation.1.clone.clone.1 | custom fusion | bytes 8650752 | tf_op jit(solution)/shard_map/while/body/eval_jaxpr/gather | solution.py:68
  603.7 35.9 %psum.36 = bf16[64,256]{1,0:T(8,128)(2,1)S(1)} all-reduce(f32[64,256]{1,0:T(8,128)S(1)} %get-tuple-element.122), channel_id=1, replica_groups=mesh['comp'=8,'band'=16] {'comp'}, use_global_device_ids=true, to_apply=%region_4.5 | all-reduce | flops 16384 | bytes 98304 | tf_op jit(solution)/shard_map/psum | solution.py:95
  654.3 591.4 %while.27 = (s32[]{:T(128)}, f32[64,256]{1,0:T(8,128)S(1)}, f32[4,64,256]{2,1,0:T(8,128)S(1)}, bf16[128,256]{1,0:T(8,128)(2,1)S(1)}, bf16[4,65,65]{1,2,0:T(8,128)(2,1)S(1)}, /*index=5*/s32[]{:T(128)}, s32[]{:T(128)}) while((s32[]{:T(128)}, f32[64,256]{1,0:T(8,128)S(1)}, f32[4,64,256]{2,1,0:T(8,128)S(1)}, ...), condition=%wide.region_6.7_spmd.clone, body=%wide.region_5.6_spmd.clone.sunk | while | flops 548050176 | bytes 44095328 | solution.py:103
  654.4 114.2 %gather_fusion.3 = bf16[32768,65]{1,0:T(8,128)(2,1)} fusion(bf16[65,65]{0,1:T(8,128)(2,1)S(1)} %dynamic-slice_bitcast_fusion.8, s32[32768]{0:T(1024)S(1)} %fusion.78), kind=kCustom, calls=%fused_computation.3.clone.clone.1 | custom fusion | bytes 8650752 | tf_op jit(solution)/shard_map/while/body/eval_jaxpr/gather | solution.py:68
  779.5 16.3 %gather_fusion.2 = bf16[4160,2,256]{2,1,0:T(2,128)(2,1)} fusion(bf16[128,2,256]{2,1,0:T(2,128)(2,1)S(1)} %pad_maximum_fusion.7, s32[5120]{0:T(1024)S(1)} %pad_clamp_fusion.5), kind=kCustom, calls=%fused_computation.2.clone.clone.1 | custom fusion | bytes 8536320 | tf_op jit(solution)/shard_map/while/body/eval_jaxpr/gather | solution.py:64
  802.3 114.2 %gather_fusion.3 = bf16[32768,65]{1,0:T(8,128)(2,1)} fusion(bf16[65,65]{0,1:T(8,128)(2,1)S(1)} %dynamic-slice_bitcast_fusion.8, s32[32768]{0:T(1024)S(1)} %fusion.78), kind=kCustom, calls=%fused_computation.3.clone.clone.1 | custom fusion | bytes 8650752 | tf_op jit(solution)/shard_map/while/body/eval_jaxpr/gather | solution.py:68
  927.4 16.3 %gather_fusion.2 = bf16[4160,2,256]{2,1,0:T(2,128)(2,1)} fusion(bf16[128,2,256]{2,1,0:T(2,128)(2,1)S(1)} %pad_maximum_fusion.7, s32[5120]{0:T(1024)S(1)} %pad_clamp_fusion.5), kind=kCustom, calls=%fused_computation.2.clone.clone.1 | custom fusion | bytes 8536320 | tf_op jit(solution)/shard_map/while/body/eval_jaxpr/gather | solution.py:64
  950.1 114.2 %gather_fusion.3 = bf16[32768,65]{1,0:T(8,128)(2,1)} fusion(bf16[65,65]{0,1:T(8,128)(2,1)S(1)} %dynamic-slice_bitcast_fusion.8, s32[32768]{0:T(1024)S(1)} %fusion.78), kind=kCustom, calls=%fused_computation.3.clone.clone.1 | custom fusion | bytes 8650752 | tf_op jit(solution)/shard_map/while/body/eval_jaxpr/gather | solution.py:68
  1064.3 10.6 copy.69
  1075.2 16.3 %gather_fusion.2 = bf16[4160,2,256]{2,1,0:T(2,128)(2,1)} fusion(bf16[128,2,256]{2,1,0:T(2,128)(2,1)S(1)} %pad_maximum_fusion.7, s32[5120]{0:T(1024)S(1)} %pad_clamp_fusion.5), kind=kCustom, calls=%fused_computation.2.clone.clone.1 | custom fusion | bytes 8536320 | tf_op jit(solution)/shard_map/while/body/eval_jaxpr/gather | solution.py:64
  1097.9 114.2 %gather_fusion.3 = bf16[32768,65]{1,0:T(8,128)(2,1)} fusion(bf16[65,65]{0,1:T(8,128)(2,1)S(1)} %dynamic-slice_bitcast_fusion.8, s32[32768]{0:T(1024)S(1)} %fusion.78), kind=kCustom, calls=%fused_computation.3.clone.clone.1 | custom fusion | bytes 8650752 | tf_op jit(solution)/shard_map/while/body/eval_jaxpr/gather | solution.py:68
  1212.1 10.6 copy.69
  1223.1 16.3 %gather_fusion.2 = bf16[4160,2,256]{2,1,0:T(2,128)(2,1)} fusion(bf16[128,2,256]{2,1,0:T(2,128)(2,1)S(1)} %pad_maximum_fusion.7, s32[5120]{0:T(1024)S(1)} %pad_clamp_fusion.5), kind=kCustom, calls=%fused_computation.2.clone.clone.1 | custom fusion | bytes 8536320 | tf_op jit(solution)/shard_map/while/body/eval_jaxpr/gather | solution.py:64
  1246.5 77.4 %all-reduce.6.cloned.1.call-done = f32[64,256]{0,1:T(8,128)} async-done(((f32[64,256]{0,1:T(8,128)}), f32[64,256]{0,1:T(8,128)}) %all-reduce.6.cloned.1.call-update) | async-done | bytes 65552 | tf_op jit(solution)/shard_map/psum | solution.py:106
  1325.6 33.2 %all-reduce.3 = (f32[]{:T(128)}, f32[]{:T(128)}) all-reduce(f32[]{:T(128)} %multiply_reduce_fusion.2, f32[]{:T(128)} %multiply_reduce_fusion.1), channel_id=1, replica_groups=mesh['comp'=8,'band'=16] {'band'}, use_global_device_ids=true, to_apply=%region_1.2 | all-reduce | flops 2 | bytes 16 | tf_op jit(solution)/shard_map/psum | solution.py:108
  1361.6 27.8 %psum.39 = f32[]{:T(128)} all-reduce(f32[]{:T(128)} %get-tuple-element.193), channel_id=1, replica_groups=mesh['comp'=8,'band'=16] {'band'}, use_global_device_ids=true, to_apply=%region_11.12 | all-reduce | flops 1 | bytes 8 | tf_op jit(solution)/shard_map/psum | solution.py:112
  (179 shorter events, 152.7 us)
Async XLA Ops:
  7.2 1316.8 %all-reduce.6.cloned.1.call-start = ((), (), s32[]{:S(2)}) async-start(), calls=%async_computation | async-start | bytes 262144 | tf_op jit(solution)/shard_map/psum | solution.py:106
  8.2 9.0 collective-permute-start
  12.8 5.6 collective-permute-start.1
  18.4 633.3 %copy-start = (bf16[4,64,256]{2,1,0:T(8,128)(2,1)S(1)}, bf16[4,64,256]{2,1,0:T(8,128)(2,1)}, u32[]{:S(2)}) copy-start(bf16[4,64,256]{2,1,0:T(8,128)(2,1)} %param.16) | copy-start | bytes 393220
  18.4 633.3 %copy-start.1 = (f32[64,256]{1,0:T(8,128)S(1)}, f32[64,256]{1,0:T(8,128)}, u32[]{:S(2)}) copy-start(f32[64,256]{1,0:T(8,128)} %param.14) | copy-start | bytes 196612
  18.4 633.4 %copy-start.2 = (f32[64,256]{1,0:T(8,128)S(1)}, f32[64,256]{1,0:T(8,128)}, u32[]{:S(2)}) copy-start(f32[64,256]{1,0:T(8,128)} %param.13) | copy-start | bytes 196612
  639.6 12.4 collective-permute-start.2
  649.2 5.1 collective-permute-start.3
  654.3 671.2 %copy-start.3 = (f32[64,256]{1,0:T(8,128)S(1)}, f32[64,256]{1,0:T(8,128)}, u32[]{:S(2)}) copy-start(f32[64,256]{1,0:T(8,128)} %param.12) | copy-start | bytes 196612
  654.3 741.0 %copy-start.4 = (f32[64,3,3]{0,2,1:T(4,128)S(1)}, f32[64,3,3]{0,2,1:T(4,128)}, u32[]{:S(2)}) copy-start(f32[64,3,3]{0,2,1:T(4,128)} %param.17) | copy-start | bytes 6916
  654.3 741.0 %copy-start.5 = (f32[64,3,3]{0,2,1:T(4,128)S(1)}, f32[64,3,3]{0,2,1:T(4,128)}, u32[]{:S(2)}) copy-start(f32[64,3,3]{0,2,1:T(4,128)} %param.19) | copy-start | bytes 6916
  654.3 745.3 %copy-start.6 = (f32[64]{0:T(128)S(1)}, f32[64]{0:T(128)}, u32[]{:S(2)}) copy-start(f32[64]{0:T(128)} %param.18) | copy-start | bytes 772
  1390.9 6.6 collective-permute-start.4
  1392.8 6.3 collective-permute-start.5
Sparse Core Ops, SparseCore 0:
  1246.6 77.2 all-reduce.5
where the time goes:
time: 1410 us
  local copies, waits for them, and re-layouts  1150 us (82%)
  blocking collectives  96.8 us (7%)
  waiting for transfers between devices  82.6 us (6%)
  matrix products  35 us (2%)
  starting transfers between devices  22.5 us (2%)
  between operations  17 us (1%)
    gather x16, local copies, waits for them, and re-layouts, correlate(): taps[:, jnp.clip(spacing, 0, span - 1)]  998 us
    gather x12, local copies, waits for them, and re-layouts, correlate(): stacked = blocks[offsets]  141 us
    psum x1, waiting for transfers between devices, per_device(): normal = lax.psum(local_sum, 'comp')  77.4 us
    psum x1, blocking collectives, per_device(): image = lax.psum(partial_value, 'comp').astype(jnp.bfloat16)  35.9 us
    dot_general x8, matrix products, correlate(): jnp.einsum('arnu,auv->rnv', stacked, toeplitz, preferred_element_type=jnp...  33.2 us
    psum x1, blocking collectives, per_device(): old = lax.psum(jnp.sum(residual * residual), 'band')  33.2 us
  transfers between devices with their start and end apart: 7, of which 4 were waited for; matrix products, arithmetic and copies ran while one was open for 0% of the time, Pallas kernels for 0%

commit v1 on v0

v1 whole, which is shorter than its diff:
```python
import functools

import jax
import jax.numpy as jnp
from jax import lax
from jax.experimental import pallas as pl
from jax.experimental.pallas import tpu as pltpu
from jax.sharding import PartitionSpec as P

MESH = pl.DeviceIdType.MESH
F32 = jnp.float32
BF16 = jnp.bfloat16
DAMPING = 0.5
HALF = 32
SPAN = 65
ROWS = 64
WIDTH = 256
FINE = 4
COARSE = 8
GROUP = 40


def lane_shift(x, n):
    if n == 0:
        return x
    width = x.shape[1]
    col = lax.broadcasted_iota(jnp.int32, x.shape, 1)
    keep = col < width - n if n > 0 else col >= -n
    return jnp.where(keep, pltpu.roll(x, (-n) % width, 1), 0.0)


def fold(x):
    x = jnp.sum(x, axis=0, keepdims=True)
    return x[:, :128] + x[:, 128:]


def remote(src, dst, send, recv, comp, band):
    return pltpu.make_async_remote_copy(
        src_ref=src, dst_ref=dst, send_sem=send, recv_sem=recv,
        device_id=(comp, band), device_id_type=MESH,
    )


def kernel(
    nc, nb, unroll,
    est_ref, res_ref, dir_ref, ker_ref, w_ref, fin_ref, bias_ref, fout_ref,
    en_ref, rn_ref, dn_ref, den_ref,
    own, halo, edge, edge_halo, kscr, kt, ktj, gf, gz, hb, hz, shifted, ishift, acc,
    part, rsbuf, iblk, iwin, part2, rsbuf2, sca, sca_in, ag, scb, ext,
    h_s, h_r, rs_s, rs_r, iw_s, in_s, iw_r, rt_s, rt_r, sa_s, sa_r, ag_s, ag_r, sb_s, sb_r,
):
    ci = lax.axis_index("comp")
    bi = lax.axis_index("band")
    up = lax.rem(bi + nb - 1, nb)
    down = lax.rem(bi + 1, nb)
    comps = w_ref.shape[0]

    def peers(fn):
        def body(d, carry):
            fn(lax.rem(ci + d, nc))
            return carry
        lax.fori_loop(1, nc, body, 0)

    def bands(fn):
        def body(d, carry):
            fn(lax.rem(bi + d, nb))
            return carry
        lax.fori_loop(1, nb, body, 0)

    barrier = pltpu.get_barrier_semaphore()

    def greet(comp, band):
        pl.semaphore_signal(barrier, inc=1, device_id=(comp, band), device_id_type=MESH)

    peers(lambda j: greet(j, bi))

    def greet_both(c, carry):
        greet(c, up)
        greet(c, down)
        return carry
    lax.fori_loop(0, nc, greet_both, 0)

    def greet_far(d, carry):
        greet(ci, lax.rem(bi + d, nb))
        return carry
    lax.fori_loop(2, nb - 1, greet_far, 0)

    direction = dir_ref[...]
    for k in range(comps):
        shaped = (w_ref[k].astype(F32) * direction).astype(BF16)
        own[0, k] = shaped[:HALF]
        own[1, k] = shaped[HALF:]
    edge[0, 0] = est_ref[:8]
    edge[0, 1] = dir_ref[:8]
    edge[1, 0] = est_ref[ROWS - 8:]
    edge[1, 1] = dir_ref[ROWS - 8:]

    pl.semaphore_wait(barrier, nc - 1 + 2 * nc + nb - 3)

    halos = [
        remote(own.at[0], halo.at[1], h_s.at[0], h_r.at[1], ci, up),
        remote(own.at[1], halo.at[0], h_s.at[1], h_r.at[0], ci, down),
        remote(edge.at[0], edge_halo.at[1], h_s.at[2], h_r.at[3], ci, up),
        remote(edge.at[1], edge_halo.at[0], h_s.at[3], h_r.at[2], ci, down),
    ]
    for copy in halos:
        copy.start()

    size = 128
    kscr[...] = jnp.zeros_like(kscr)
    anti_r = lax.broadcasted_iota(jnp.int32, (size, size), 0)
    anti_c = lax.broadcasted_iota(jnp.int32, (size, size), 1)
    anti = (anti_r + anti_c == SPAN - 1).astype(BF16)
    for k in range(comps):
        kscr[k, 0:SPAN, 0:SPAN] = ker_ref[k].astype(F32)
    for k in range(comps):
        turned = kscr[k].T
        kt[k] = turned
        ktj[k] = jnp.dot(turned.astype(BF16), anti, preferred_element_type=F32)

    def band_matrix(table, k, b):
        row = table[k, pl.ds(b, 1), :]
        spread = jnp.broadcast_to(row, (ROWS, 128))
        return pltpu.roll(spread, 0, 1, stride=1, stride_axis=0).astype(BF16)

    def build_forward(s1, carry):
        at = pl.ds(pl.multiple_of(s1 * ROWS, ROWS), ROWS)
        for side, sign in ((0, 1), (1, -1)):
            for s0 in range(FINE):
                b = HALF + sign * (1 + s0 + FINE * s1)
                for k in range(comps):
                    lanes = pl.ds((s0 * comps + k) * 128, 128)
                    gf[side, at, lanes] = band_matrix(kt, k, b)
        return carry
    lax.fori_loop(0, COARSE, build_forward, 0)
    for k in range(comps):
        gz[:, pl.ds(k * 128, 128)] = band_matrix(kt, k, HALF)

    def all_shifts(x):
        x = x.astype(F32)
        yield 0, x.astype(BF16)
        for s0 in range(FINE):
            yield 1 + s0, lane_shift(x, 1 + s0).astype(BF16)
            yield 1 + FINE + s0, lane_shift(x, -1 - s0).astype(BF16)

    def shift_own(k, carry):
        for h in range(2):
            for at, value in all_shifts(own[h, k]):
                shifted[at, k, pl.ds(HALF * (1 + h), HALF), :] = value
        return carry
    lax.fori_loop(0, comps, shift_own, 0)

    for copy in halos:
        copy.wait_recv()
    inside = ((bi > 0).astype(F32), (bi < nb - 1).astype(F32))

    def shift_halo(k, carry):
        for h in range(2):
            for at, value in all_shifts(halo[h, k].astype(F32) * inside[h]):
                shifted[at, k, pl.ds(96 * h, HALF), :] = value
        return carry
    lax.fori_loop(0, comps, shift_halo, 0)

    depth = comps * 128
    total = jnp.dot(
        gz[...], shifted[0].reshape(depth, WIDTH), preferred_element_type=F32)
    for side, sign in ((0, 1), (1, -1)):
        source = shifted[pl.ds(1 + side * FINE, FINE)].reshape(FINE * depth, WIDTH)
        acc[...] = jnp.dot(gf[side], source, preferred_element_type=F32)
        for s1 in range(COARSE):
            total += lane_shift(acc[pl.ds(s1 * ROWS, ROWS), :], sign * FINE * s1)
    for j in range(8):
        r, c = j // 2, j % 2
        part[j] = total[16 * r:16 * r + 16, 128 * c:128 * c + 128]

    def rs(j, slot):
        return remote(part.at[j], rsbuf.at[slot], rs_s.at[j], rs_r.at[slot], j, bi)
    peers(lambda j: rs(j, ci).start())

    def build_back(s1, carry):
        at = pl.ds(pl.multiple_of(s1 * ROWS, ROWS), ROWS)
        for side, sign in ((0, 1), (1, -1)):
            for s0 in range(FINE):
                b = HALF - sign * (1 + s0 + FINE * s1)
                for k in range(comps):
                    hb[side, k, at, pl.ds(s0 * 128, 128)] = band_matrix(ktj, k, b)
        return carry
    lax.fori_loop(0, COARSE, build_back, 0)
    for k in range(comps):
        hz[k] = band_matrix(ktj, k, HALF)

    rsbuf[ci] = part[ci]
    peers(lambda j: rs(j, j).wait_recv())
    block = rsbuf[0]
    for j in range(1, nc):
        block += rsbuf[j]
    iblk[...] = block.astype(BF16)
    iwin[ci + 4] = iblk[...]
    far = lax.div(ci, 4)
    far_band = lax.rem(bi + nb - 1 + 2 * far, nb)
    far_slot = ci + 12 - 16 * far

    def to_peer(j):
        return remote(iblk, iwin.at[ci + 4], iw_s.at[j], iw_r.at[ci + 4], j, bi)

    def to_far(j):
        return remote(iblk, iwin.at[far_slot], in_s.at[j], iw_r.at[far_slot], j, far_band)

    def start_far(j, carry):
        to_far(j).start()
        return carry
    lax.fori_loop(0, nc, start_far, 0)
    peers(lambda j: to_peer(j).start())

    def window(at):
        return remote(iblk, iwin.at[at], iw_s.at[0], iw_r.at[at], ci, up)
    peers(lambda j: window(j + 4).wait_recv())

    def wait_far(j, carry):
        window(j).wait_recv()
        window(j + 12).wait_recv()
        return carry
    lax.fori_loop(0, 4, wait_far, 0)

    for r in range(8):
        pair = jnp.concatenate([iwin[2 * r].astype(F32), iwin[2 * r + 1].astype(F32)], axis=1)
        if r < 2:
            pair = pair * inside[0]
        if r >= 6:
            pair = pair * inside[1]
        for at, value in all_shifts(pair):
            ishift[at, pl.ds(16 * r, 16), :] = value

    part_sum = part2
    rsum = jnp.zeros((ROWS, WIDTH), F32)
    for k in range(comps):
        back = jnp.dot(hz[k], ishift[0], preferred_element_type=F32)
        for side, sign in ((0, 1), (1, -1)):
            source = ishift[pl.ds(1 + side * FINE, FINE)].reshape(FINE * 128, WIDTH)
            acc[...] = jnp.dot(hb[side, k], source, preferred_element_type=F32)
            for s1 in range(COARSE):
                back += lane_shift(acc[pl.ds(s1 * ROWS, ROWS), :], sign * FINE * s1)
        rsum += w_ref[k].astype(F32) * back
    for j in range(8):
        r, c = j // 2, j % 2
        part_sum[j] = rsum[16 * r:16 * r + 16, 128 * c:128 * c + 128]

    def rt(j, slot):
        return remote(part_sum.at[j], rsbuf2.at[slot], rt_s.at[j], rt_r.at[slot], j, bi)
    peers(lambda j: rt(j, ci).start())

    direction = dir_ref[...]
    residual = res_ref[...]
    sca[...] = jnp.zeros_like(sca)
    sca[0:1] = fold(direction * rsum)
    sca[1:2] = fold(direction * direction)
    sca[2:3] = fold(residual * residual)

    def sa(b, slot):
        return remote(sca, sca_in.at[slot], sa_s.at[b], sa_r.at[slot], ci, b)
    bands(lambda b: sa(b, bi).start())
    sca_in[bi] = sca[...]
    rsbuf2[ci] = part_sum[ci]

    peers(lambda j: rt(j, j).wait_recv())
    block = rsbuf2[0]
    for j in range(1, nc):
        block += rsbuf2[j]
    bands(lambda b: sa(b, b).wait_recv())
    scalars = sca_in[0]
    for b in range(1, nb):
        scalars += sca_in[b]
    ag[ci, 0:16] = block
    ag[ci, 16:24] = scalars

    def gather(j, slot):
        return remote(ag.at[ci], ag.at[slot], ag_s.at[j], ag_r.at[slot], j, bi)
    peers(lambda j: gather(j, ci).start())
    peers(lambda j: gather(j, j).wait_recv())

    product = ag[0, 16:17]
    for j in range(1, nc):
        product += ag[j, 16:17]
    product = product + DAMPING * ag[0, 17:18]
    old = jnp.sum(ag[0, 18:19], axis=1, keepdims=True)
    alpha = old / jnp.sum(product, axis=1, keepdims=True)

    for j in range(8):
        r, c = j // 2, j % 2
        at = (slice(16 * r, 16 * r + 16), slice(128 * c, 128 * c + 128))
        rn_ref[at] = res_ref[at] - alpha * (ag[j, 0:16] + DAMPING * dir_ref[at])
    updated = rn_ref[...]
    scb[nb] = jnp.broadcast_to(fold(updated * updated), (8, 128))

    def sb(b, slot):
        return remote(scb.at[nb], scb.at[slot], sb_s.at[b], sb_r.at[slot], ci, b)
    bands(lambda b: sb(b, bi).start())
    scb[bi] = scb[nb]

    estimate_next = est_ref[...] + alpha * dir_ref[...]
    en_ref[...] = estimate_next
    ext[0:8] = (edge_halo[0, 0] + alpha * edge_halo[0, 1]) * inside[0]
    ext[8:72] = estimate_next
    ext[72:80] = (edge_halo[1, 0] + alpha * edge_halo[1, 1]) * inside[1]
    framed = ext[...]
    columns = WIDTH // nc
    start = ci * columns
    pick_r = lax.broadcasted_iota(jnp.int32, (WIDTH, 128), 0)
    pick_c = lax.broadcasted_iota(jnp.int32, (WIDTH, 128), 1)
    group = (pick_c >= GROUP).astype(jnp.int32) + (pick_c >= 2 * GROUP).astype(jnp.int32)
    pick = (pick_r == start - 2 + pick_c - GROUP * group).astype(BF16)
    high = framed.astype(BF16)
    rest = framed - high.astype(F32)
    middle = rest.astype(BF16)
    low = (rest - middle.astype(F32)).astype(BF16)
    tile = (
        jnp.dot(high, pick, preferred_element_type=F32)
        + jnp.dot(middle, pick, preferred_element_type=F32)
        + jnp.dot(low, pick, preferred_element_type=F32)
    )
    tile = jnp.concatenate([tile[6:80], jnp.zeros((14, 128), F32)], axis=0)
    lane = lax.broadcasted_iota(jnp.int32, (24, 128), 1)
    row = lax.broadcasted_iota(jnp.int32, (24, 128), 0)
    third = (lane >= GROUP).astype(jnp.int32) + (lane >= 2 * GROUP).astype(jnp.int32)
    taps = []
    for a in range(3):
        packed = jnp.where(
            third == 0, tile[a:a + 24], jnp.where(third == 1, tile[24 + a:48 + a], tile[48 + a:72 + a]))
        for b in range(3):
            taps.append(packed if b == 0 else pltpu.roll(packed, 128 - b, 1))
    image_row = bi * ROWS - 1 + row + 24 * third
    image_col = start - 1 + lane - GROUP * third
    valid = (image_row >= 0) & (image_row < nb * ROWS) & (image_col >= 0) & (image_col < WIDTH)
    channels = bias_ref.shape[0]
    spreads = []
    for part_of in range(3):
        rows = slice(8 * part_of, 8 * part_of + 8)
        mine = [tap[rows] for tap in taps]

        def channel(c, sums):
            value = mine[0] * fin_ref[c * 9] + bias_ref[c]
            for t in range(1, 9):
                value += mine[t] * fin_ref[c * 9 + t]
            value = jnp.maximum(value, 0.0)
            return tuple(sums[t] + value * fout_ref[c * 9 + t] for t in range(9))

        sums = lax.fori_loop(
            0, channels, channel, tuple(jnp.zeros((8, 128), F32) for t in range(9)), unroll=unroll)
        spreads.append(sums)
    mixed = jnp.zeros((ROWS, 128), F32)
    for t in range(9):
        a, b = t // 3, t % 3
        whole = jnp.where(valid, jnp.concatenate([s[t] for s in spreads], axis=0), 0.0)
        column = jnp.concatenate(
            [pltpu.roll(whole, (128 - GROUP * g - b) % 128, 1) for g in range(3)], axis=0)
        mixed += column[a:a + ROWS]
    centre = pltpu.roll(tile[2:2 + ROWS], 126, 1)
    den_ref[...] = (centre - mixed)[:, :columns]

    bands(lambda b: sb(b, b).wait_recv())
    new = scb[0, 0:1]
    for b in range(1, nb):
        new += scb[b, 0:1]
    new = jnp.sum(new, axis=1, keepdims=True)
    dn_ref[...] = rn_ref[...] + (new / old) * dir_ref[...]

    for copy in halos:
        copy.wait_send()
    peers(lambda j: rs(j, ci).wait_send())
    peers(lambda j: to_peer(j).wait_send())

    def end_far(j, carry):
        to_far(j).wait_send()
        return carry
    lax.fori_loop(0, nc, end_far, 0)
    peers(lambda j: rt(j, ci).wait_send())
    bands(lambda b: sa(b, bi).wait_send())
    peers(lambda j: gather(j, ci).wait_send())
    bands(lambda b: sb(b, bi).wait_send())


def per_device(nc, nb, unroll, estimate, residual, direction, kernels, weight_maps, filters_in, biases, filters_out):
    comps = weight_maps.shape[0]
    columns = WIDTH // nc
    vmem = pl.BlockSpec(memory_space=pltpu.VMEM)
    smem = pl.BlockSpec(memory_space=pltpu.SMEM)
    band = jax.ShapeDtypeStruct((ROWS, WIDTH), F32)
    dma = pltpu.SemaphoreType.DMA
    return pl.pallas_call(
        functools.partial(kernel, nc, nb, unroll),
        out_shape=(band, band, band, jax.ShapeDtypeStruct((ROWS, columns), F32)),
        in_specs=[vmem] * 5 + [smem] * 3,
        out_specs=(vmem,) * 4,
        scratch_shapes=[
            pltpu.VMEM((2, comps, HALF, WIDTH), BF16),
            pltpu.VMEM((2, comps, HALF, WIDTH), BF16),
            pltpu.VMEM((2, 2, 8, WIDTH), F32),
            pltpu.VMEM((2, 2, 8, WIDTH), F32),
            pltpu.VMEM((comps, 128, 128), F32),
            pltpu.VMEM((comps, 128, 128), F32),
            pltpu.VMEM((comps, 128, 128), F32),
            pltpu.VMEM((2, COARSE * ROWS, FINE * comps * 128), BF16),
            pltpu.VMEM((ROWS, comps * 128), BF16),
            pltpu.VMEM((2, comps, COARSE * ROWS, FINE * 128), BF16),
            pltpu.VMEM((comps, ROWS, 128), BF16),
            pltpu.VMEM((1 + 2 * FINE, comps, 128, WIDTH), BF16),
            pltpu.VMEM((1 + 2 * FINE, 128, WIDTH), BF16),
            pltpu.VMEM((COARSE * ROWS, WIDTH), F32),
            pltpu.VMEM((8, 16, 128), F32),
            pltpu.VMEM((8, 16, 128), F32),
            pltpu.VMEM((16, 128), BF16),
            pltpu.VMEM((16, 16, 128), BF16),
            pltpu.VMEM((8, 16, 128), F32),
            pltpu.VMEM((8, 16, 128), F32),
            pltpu.VMEM((8, 128), F32),
            pltpu.VMEM((nb, 8, 128), F32),
            pltpu.VMEM((nc, 24, 128), F32),
            pltpu.VMEM((nb + 1, 8, 128), F32),
            pltpu.VMEM((80, WIDTH), F32),
            dma((4,)), dma((4,)),
            dma((nc,)), dma((nc,)),
            dma((nc,)), dma((nc,)), dma((16,)),
            dma((nc,)), dma((nc,)),
            dma((nb,)), dma((nb,)),
            dma((nc,)), dma((nc,)),
            dma((nb,)), dma((nb,)),
        ],
        compiler_params=pltpu.CompilerParams(
            collective_id=0, has_side_effects=True, vmem_limit_bytes=48 * 1024 * 1024),
        cost_estimate=pl.CostEstimate(
            flops=4 * 65 * comps * 64 * 128 * 256, bytes_accessed=1 << 20, transcendentals=0),
    )(estimate, residual, direction, kernels, weight_maps,
      filters_in.reshape(-1), biases, filters_out.reshape(-1))


def solution(mesh):
    nc, nb = mesh.shape["comp"], mesh.shape["band"]
    return jax.shard_map(
        functools.partial(per_device, nc, nb, 4),
        mesh=mesh,
        in_specs=(
            P("band", None),
            P("band", None),
            P("band", None),
            P("comp", None, None),
            P("comp", "band", None),
            P(),
            P(),
            P(),
        ),
        out_specs=(P("band", None), P("band", None), P("band", None), P("band", "comp")),
        check_vma=False,
    )
```

time: 1410 us -> 50.8 us (0.04)
  local copies, waits for them, and re-layouts: 1150 us -> 5.26 us
  blocking collectives: 96.8 us -> 0 us
  waiting for transfers between devices: 82.6 us -> 0 us
  Pallas kernels: 0 us -> 44.6 us
  matrix products: 35 us -> 0 us
  starting transfers between devices: 22.5 us -> 0 us
  between operations: 17 us -> 0.73 us
    gather x28 -> x0, local copies, waits for them, and re-layouts: 1140 us -> none  [the longest x16 998 us: correlate(): taps[:, jnp.clip(spacing, 0, span - 1)]]
    psum x3 -> x0, blocking collectives: 96.8 us -> none  [the longest x1 35.9 us: per_device(): image = lax.psum(partial_value, 'comp').astype(jnp.bfloat16)]
    psum x1 -> x0, waiting for transfers between devices: 77.4 us -> none  [per_device(): normal = lax.psum(local_sum, 'comp')]
    pallas_call x0 -> x1, Pallas kernels: none -> 44.6 us  [per_device(): pl.pallas_call(functools.partial(kernel, nc, nb, unroll), out_shape=(band...]
    dot_general x10 -> x0, matrix products: 35 us -> none  [the longest x8 33.2 us: correlate(): jnp.einsum('arnu,auv->rnv', stacked, toeplitz, preferred_element_type=jnp...]
    ppermute x6 -> x0, starting transfers between devices: 22.4 us -> none  [the longest x3 16.2 us: with_halo(): before = lax.ppermute(last, axis, up)]
  transfers between devices with their start and end apart: 7 -> 0, of which waited for: 4 -> 0; matrix products, arithmetic and copies ran while one was open for 0% -> 0% of each run, Pallas kernels for 0% -> 0%
where the time goes in v1:
time: 50.8 us; the launch traced here: 50.6 us
  Pallas kernels  44.6 us (88%)
  local copies, waits for them, and re-layouts  5.26 us (10%)
  between operations  0.73 us (1%)
    pallas_call x1, Pallas kernels, per_device(): pl.pallas_call(functools.partial(kernel, nc, nb, unroll), out_shape=(band...  44.6 us
    unnamed x20, local copies, waits for them, and re-layouts  4.16 us

profile of v1, /device:TPU:1, one launch (start us, length us, event | category | flops | bytes accessed | tf_op | source)
XLA Modules:
  0.0 50.6 jit_solution(13016177380709158877)
XLA Ops:
  0.6 0.0 copy-start.5
  0.6 0.9 %copy.16.ker_ref = bf16[4,65,65]{2,1,0:T(8,128)(2,1)S(1)} copy(bf16[4,65,65]{2,0,1:T(4,128)(2,1)} %param.11) | data formatting | bytes 67600 | tf_op args[3]
  1.5 0.0 copy-done.5
  1.6 0.1 copy.14
  1.7 0.0 copy-start.6
  1.7 0.0 copy-start.3
  1.7 0.2 reshape.14.fin_ref
  1.9 0.5 copy-done.6
  2.4 0.0 copy-start
  2.4 0.1 copy.15
  2.5 0.0 copy-start.1
  2.5 0.0 copy-start.2
  2.5 0.0 copy-start.4
  2.6 0.2 reshape.15.fout_ref
  2.8 0.0 copy-done.3
  2.8 0.5 %copy-done = bf16[4,64,256]{2,1,0:T(8,128)(2,1)S(1)} copy-done((bf16[4,64,256]{2,1,0:T(8,128)(2,1)S(1)}, bf16[4,64,256]{2,1,0:T(8,128)(2,1)}, u32[]{:S(2)}) %copy-start) | copy-done | bytes 131096
  3.3 0.1 copy-done.1
  3.4 0.0 copy-done.2
  3.4 0.0 copy-done.4
  3.4 44.6 %shard_map.111 = (f32[64,256]{1,0:T(8,128)S(1)}, f32[64,256]{1,0:T(8,128)S(1)}, f32[64,256]{1,0:T(8,128)S(1)}, f32[64,32]{1,0:T(8,128)S(1)}) custom-call(f32[64,256]{1,0:T(8,128)S(1)} %copy-done.1, f32[64,256]{1,0:T(8,128)S(1)} %copy-done.2, f32[64,256]{1,0:T(8,128)S(1)} %copy-done.3, bf16[4,65,65]{2,1,0:T(8,128)(2,1)S(1)} %copy.16.ker_ref, ...), custom_call_target="tpu_custom_call" | custom-call | flops 2181038080 | bytes 1048576 | tf_op jit(solution)/shard_map/pallas_call | solution.py:389
  48.0 0.7 %copy.17 = f32[64,32]{0,1:T(8,128)} copy(f32[64,32]{1,0:T(8,128)S(1)} %get-tuple-element.11) | data formatting | bytes 16384 | tf_op jit(solution)/shard_map/pallas_call | solution.py:389
  48.7 0.6 %copy.21 = f32[64,256]{1,0:T(8,128)} copy(f32[64,256]{1,0:T(8,128)S(1)} %get-tuple-element.16) | data formatting | bytes 131072
  49.3 0.6 %copy.22 = f32[64,256]{1,0:T(8,128)} copy(f32[64,256]{1,0:T(8,128)S(1)} %get-tuple-element.17) | data formatting | bytes 131072
  50.0 0.6 %copy.23 = f32[64,256]{1,0:T(8,128)} copy(f32[64,256]{1,0:T(8,128)S(1)} %get-tuple-element.18) | data formatting | bytes 131072
Async XLA Ops:
  0.6 0.9 %copy-start.5 = (f32[64,3,3]{0,2,1:T(4,128)S(1)}, f32[64,3,3]{0,2,1:T(4,128)}, u32[]{:S(2)}) copy-start(f32[64,3,3]{0,2,1:T(4,128)} %param.13) | copy-start | bytes 6916
  1.7 0.7 %copy-start.6 = (f32[64,3,3]{0,2,1:T(4,128)S(1)}, f32[64,3,3]{0,2,1:T(4,128)}, u32[]{:S(2)}) copy-start(f32[64,3,3]{0,2,1:T(4,128)} %param.15) | copy-start | bytes 6916
  1.7 1.1 %copy-start.3 = (f32[64,256]{1,0:T(8,128)S(1)}, f32[64,256]{1,0:T(8,128)}, u32[]{:S(2)}) copy-start(f32[64,256]{1,0:T(8,128)} %dir_ref.1) | copy-start | bytes 196612
  2.4 0.9 %copy-start = (bf16[4,64,256]{2,1,0:T(8,128)(2,1)S(1)}, bf16[4,64,256]{2,1,0:T(8,128)(2,1)}, u32[]{:S(2)}) copy-start(bf16[4,64,256]{2,1,0:T(8,128)(2,1)} %w_ref.1) | copy-start | bytes 393220
  2.5 0.9 %copy-start.1 = (f32[64,256]{1,0:T(8,128)S(1)}, f32[64,256]{1,0:T(8,128)}, u32[]{:S(2)}) copy-start(f32[64,256]{1,0:T(8,128)} %est_ref.1) | copy-start | bytes 196612
  2.5 0.9 %copy-start.2 = (f32[64,256]{1,0:T(8,128)S(1)}, f32[64,256]{1,0:T(8,128)}, u32[]{:S(2)}) copy-start(f32[64,256]{1,0:T(8,128)} %res_ref.1) | copy-start | bytes 196612
  2.5 0.9 %copy-start.4 = (f32[64]{0:T(128)S(1)}, f32[64]{0:T(128)}, u32[]{:S(2)}) copy-start(f32[64]{0:T(128)} %bias_ref.1) | copy-start | bytes 772

commit v2 on v1

v2 whole, which is shorter than its diff:
```python
import functools

import jax
import jax.numpy as jnp
from jax import lax
from jax.experimental import pallas as pl
from jax.experimental.pallas import tpu as pltpu
from jax.sharding import PartitionSpec as P

MESH = pl.DeviceIdType.MESH
F32 = jnp.float32
BF16 = jnp.bfloat16
DAMPING = 0.5
HALF = 32
SPAN = 65
ROWS = 64
WIDTH = 256
FINE = 8
COARSE = 4
GROUP = 40


def lane_shift(x, n):
    if n == 0:
        return x
    width = x.shape[1]
    col = lax.broadcasted_iota(jnp.int32, x.shape, 1)
    keep = col < width - n if n > 0 else col >= -n
    return jnp.where(keep, pltpu.roll(x, (-n) % width, 1), jnp.zeros((), x.dtype))


def fold(x):
    x = jnp.sum(x, axis=0, keepdims=True)
    return x[:, :128] + x[:, 128:]


def all_shifts(x):
    yield 0, x
    for s0 in range(FINE):
        yield 1 + s0, lane_shift(x, 1 + s0)
        yield 1 + FINE + s0, lane_shift(x, -1 - s0)


def loop(low, high, fn):
    def body(i, carry):
        fn(i)
        return carry
    lax.fori_loop(low, high, body, 0)


def remote(src, dst, send, recv, comp, band):
    return pltpu.make_async_remote_copy(
        src_ref=src, dst_ref=dst, send_sem=send, recv_sem=recv,
        device_id=(comp, band), device_id_type=MESH,
    )


def kernel(
    nc, nb, unroll,
    est_ref, res_ref, dir_ref, ker_ref, w_ref, fin_ref, bias_ref, fout_ref,
    en_ref, rn_ref, dn_ref, den_ref,
    edge, edge_halo, kscr, kt, ktj, gf, gz, hb, hz, shifted, ishift, acc,
    part, rsbuf, iblk, iwin, part2, rsbuf2, sca, sca_in, ag, scb, ext,
    h_s, h_r, rs_s, rs_r, iw_s, in_s, iw_r, rt_s, rt_r, sa_s, sa_r, ag_s, ag_r, sb_s, sb_r,
):
    ci = lax.axis_index("comp")
    bi = lax.axis_index("band")
    up = lax.rem(bi + nb - 1, nb)
    down = lax.rem(bi + 1, nb)
    comps = w_ref.shape[0]
    half_nc = nc // 2

    def peers(fn):
        loop(1, nc, lambda d: fn(lax.rem(ci + d, nc)))

    def bands(fn):
        loop(1, nb, lambda d: fn(lax.rem(bi + d, nb)))

    barrier = pltpu.get_barrier_semaphore()

    def greet(comp, band):
        pl.semaphore_signal(barrier, inc=1, device_id=(comp, band), device_id_type=MESH)

    def greet_both(c):
        greet(c, up)
        greet(c, down)
    loop(0, nc, greet_both)
    peers(lambda j: greet(j, bi))
    loop(2, nb - 1, lambda d: greet(ci, lax.rem(bi + d, nb)))

    direction = dir_ref[...]
    for k in range(comps):
        shaped = (w_ref[k].astype(F32) * direction).astype(BF16)
        for at, value in all_shifts(shaped):
            shifted[at, pl.ds(k * ROWS, ROWS), :] = value
    edge[0, 0] = est_ref[:8]
    edge[0, 1] = dir_ref[:8]
    edge[1, 0] = est_ref[ROWS - 8:]
    edge[1, 1] = dir_ref[ROWS - 8:]
    residual = res_ref[...]
    sca[...] = jnp.zeros_like(sca)
    sca[1:2] = fold(direction * direction)
    sca[2:3] = fold(residual * residual)

    size = 128
    kscr[...] = jnp.zeros_like(kscr)
    anti_r = lax.broadcasted_iota(jnp.int32, (size, size), 0)
    anti_c = lax.broadcasted_iota(jnp.int32, (size, size), 1)
    anti = (anti_r + anti_c == SPAN - 1).astype(BF16)
    for k in range(comps):
        kscr[k, 0:SPAN, 0:SPAN] = ker_ref[k].astype(F32)
    for k in range(comps):
        turned = kscr[k].T
        kt[k] = turned
        ktj[k] = jnp.dot(turned.astype(BF16), anti, preferred_element_type=F32)

    def band_matrix(table, k, b, first=0):
        row = table[k, pl.ds(b, 1), :]
        spread = jnp.broadcast_to(row, (ROWS, 128))
        return pltpu.roll(spread, first, 1, stride=1, stride_axis=0)

    left = lax.broadcasted_iota(jnp.int32, (ROWS, 128), 1) < ROWS

    def forward_pair(k, b):
        even = band_matrix(kt, k, b)
        odd = band_matrix(kt, k + 1, b, ROWS)
        lower = jnp.where(left, even, odd).astype(BF16)
        upper = jnp.where(left, odd, even).astype(BF16)
        return lower, upper

    def build_forward(s1):
        at = pl.ds(pl.multiple_of(s1 * ROWS, ROWS), ROWS)
        for side, sign in ((0, 1), (1, -1)):
            for s0 in range(FINE):
                b = HALF + sign * (1 + s0 + FINE * s1)
                for k in range(0, comps, 2):
                    lanes = pl.ds(s0 * comps * ROWS + k * ROWS, 128)
                    gf[side, 0, at, lanes], gf[side, 1, at, lanes] = forward_pair(k, b)
    loop(0, COARSE, build_forward)
    for k in range(0, comps, 2):
        gz[0, :, pl.ds(k * ROWS, 128)], gz[1, :, pl.ds(k * ROWS, 128)] = forward_pair(k, HALF)

    depth = comps * ROWS

    def taken(at, where):
        if where == 0:
            return shifted[at]
        return jnp.concatenate(
            [shifted[at, pl.ds((k ^ 1) * ROWS, ROWS), :] for k in range(comps)], axis=0)

    for where in range(2):
        total = jnp.dot(gz[where], taken(0, where), preferred_element_type=F32)
        for side, sign in ((0, 1), (1, -1)):
            source = jnp.concatenate(
                [taken(1 + side * FINE + s0, where) for s0 in range(FINE)], axis=0)
            acc[...] = jnp.dot(gf[side, where], source, preferred_element_type=F32)
            for s1 in range(COARSE):
                total += lane_shift(acc[pl.ds(s1 * ROWS, ROWS), :], sign * FINE * s1)
        base = 8 * (1 - where)
        for q in range(8):
            part[base + q] = total[8 * q:8 * q + 8]

    pl.semaphore_wait(barrier, nc - 1 + 2 * nc + nb - 3)

    def rs_up(c):
        return remote(part.at[c], rsbuf.at[nc + ci], rs_s.at[c], rs_r.at[nc + ci], c + half_nc, up)

    def rs_down(c):
        return remote(
            part.at[12 + c], rsbuf.at[nc + ci], rs_s.at[12 + c], rs_r.at[nc + ci], c, down)

    def rs(j):
        return remote(part.at[4 + j], rsbuf.at[ci], rs_s.at[4 + j], rs_r.at[ci], j, bi)

    def rs_in(slot):
        return remote(part.at[0], rsbuf.at[slot], rs_s.at[0], rs_r.at[slot], ci, up)

    def start_far(c):
        rs_up(c).start()
        rs_down(c).start()
    loop(0, half_nc, start_far)
    peers(lambda j: rs(j).start())
    edges = [
        remote(edge.at[0], edge_halo.at[1], h_s.at[0], h_r.at[1], ci, up),
        remote(edge.at[1], edge_halo.at[0], h_s.at[1], h_r.at[0], ci, down),
    ]
    for copy in edges:
        copy.start()

    def build_back(s1):
        at = pl.ds(pl.multiple_of(s1 * ROWS, ROWS), ROWS)
        for side, sign in ((0, 1), (1, -1)):
            for s0 in range(FINE):
                b = HALF - sign * (1 + s0 + FINE * s1)
                for k in range(comps):
                    hb[side, k, at, pl.ds(s0 * 128, 128)] = band_matrix(ktj, k, b).astype(BF16)
    loop(0, COARSE, build_back)
    for k in range(comps):
        hz[k] = band_matrix(ktj, k, HALF).astype(BF16)

    rsbuf[ci] = part[4 + ci]
    peers(lambda j: rs_in(j).wait_recv())
    loop(0, nc, lambda j: rs_in(nc + j).wait_recv())
    far = lax.div(ci, half_nc)
    near = rsbuf[0]
    away = rsbuf[nc]
    for j in range(1, nc):
        near += rsbuf[j]
        away += rsbuf[nc + j]
    linked = ((bi > 0) | (far == 1)) & ((bi < nb - 1) | (far == 0))
    block = near + jnp.where(linked, away, 0.0)
    iblk[...] = block.astype(BF16).astype(F32)
    iwin[ci + 4] = iblk[...]
    far_band = lax.rem(bi + nb - 1 + 2 * far, nb)
    far_slot = ci + 12 - 16 * far

    def to_peer(j):
        return remote(iblk, iwin.at[ci + 4], iw_s.at[j], iw_r.at[ci + 4], j, bi)

    def to_far(j):
        return remote(iblk, iwin.at[far_slot], in_s.at[j], iw_r.at[far_slot], j, far_band)
    loop(0, nc, lambda j: to_far(j).start())
    peers(lambda j: to_peer(j).start())

    def window(at):
        return remote(iblk, iwin.at[at], iw_s.at[0], iw_r.at[at], ci, up)
    peers(lambda j: window(j + 4).wait_recv())

    def wait_far(j):
        window(j).wait_recv()
        window(j + 12).wait_recv()
    loop(0, 4, wait_far)

    inside = ((bi > 0).astype(F32), (bi < nb - 1).astype(F32))
    for r in range(0, 16, 2):
        pair = jnp.concatenate([iwin[r], iwin[r + 1]], axis=0)
        if r < 4:
            pair = pair * inside[0]
        if r >= 12:
            pair = pair * inside[1]
        for at, value in all_shifts(pair.astype(BF16)):
            ishift[at, pl.ds(8 * r, 16), :] = value

    rsum = jnp.zeros((ROWS, WIDTH), F32)
    for k in range(comps):
        back = jnp.dot(hz[k], ishift[0], preferred_element_type=F32)
        for side, sign in ((0, 1), (1, -1)):
            source = ishift[pl.ds(1 + side * FINE, FINE)].reshape(FINE * 128, WIDTH)
            acc[...] = jnp.dot(hb[side, k], source, preferred_element_type=F32)
            for s1 in range(COARSE):
                back += lane_shift(acc[pl.ds(s1 * ROWS, ROWS), :], sign * FINE * s1)
        rsum += w_ref[k].astype(F32) * back
    for j in range(8):
        part2[j] = rsum[8 * j:8 * j + 8]

    def rt(j, slot):
        return remote(part2.at[j], rsbuf2.at[slot], rt_s.at[j], rt_r.at[slot], j, bi)
    peers(lambda j: rt(j, ci).start())
    sca[0:1] = fold(dir_ref[...] * rsum)

    def sa(b, slot):
        return remote(sca, sca_in.at[slot], sa_s.at[b], sa_r.at[slot], ci, b)
    bands(lambda b: sa(b, bi).start())
    sca_in[bi] = sca[...]
    rsbuf2[ci] = part2[ci]

    peers(lambda j: rt(j, j).wait_recv())
    block = rsbuf2[0]
    for j in range(1, nc):
        block += rsbuf2[j]
    bands(lambda b: sa(b, b).wait_recv())
    scalars = sca_in[0]
    for b in range(1, nb):
        scalars += sca_in[b]
    ag[ci, 0] = block[:, :128]
    ag[ci, 1] = block[:, 128:]
    ag[ci, 2] = scalars

    def gather(j, slot):
        return remote(ag.at[ci], ag.at[slot], ag_s.at[j], ag_r.at[slot], j, bi)
    peers(lambda j: gather(j, ci).start())
    peers(lambda j: gather(j, j).wait_recv())

    product = ag[0, 2, 0:1]
    for j in range(1, nc):
        product += ag[j, 2, 0:1]
    product = product + DAMPING * ag[0, 2, 1:2]
    old = jnp.sum(ag[0, 2, 2:3], axis=1, keepdims=True)
    alpha = old / jnp.sum(product, axis=1, keepdims=True)

    for j in range(8):
        for c in range(2):
            at = (slice(8 * j, 8 * j + 8), slice(128 * c, 128 * c + 128))
            rn_ref[at] = res_ref[at] - alpha * (ag[j, c] + DAMPING * dir_ref[at])
    updated = rn_ref[...]
    scb[nb] = jnp.broadcast_to(fold(updated * updated), (8, 128))

    def sb(b, slot):
        return remote(scb.at[nb], scb.at[slot], sb_s.at[b], sb_r.at[slot], ci, b)
    bands(lambda b: sb(b, bi).start())
    scb[bi] = scb[nb]
    for copy in edges:
        copy.wait_recv()

    estimate_next = est_ref[...] + alpha * dir_ref[...]
    en_ref[...] = estimate_next
    ext[0:8] = (edge_halo[0, 0] + alpha * edge_halo[0, 1]) * inside[0]
    ext[8:72] = estimate_next
    ext[72:80] = (edge_halo[1, 0] + alpha * edge_halo[1, 1]) * inside[1]
    framed = ext[...]
    columns = WIDTH // nc
    start = ci * columns
    pick_r = lax.broadcasted_iota(jnp.int32, (WIDTH, 128), 0)
    pick_c = lax.broadcasted_iota(jnp.int32, (WIDTH, 128), 1)
    group = (pick_c >= GROUP).astype(jnp.int32) + (pick_c >= 2 * GROUP).astype(jnp.int32)
    pick = (pick_r == start - 2 + pick_c - GROUP * group).astype(BF16)
    high = framed.astype(BF16)
    rest = framed - high.astype(F32)
    middle = rest.astype(BF16)
    low = (rest - middle.astype(F32)).astype(BF16)
    tile = (
        jnp.dot(high, pick, preferred_element_type=F32)
        + jnp.dot(middle, pick, preferred_element_type=F32)
        + jnp.dot(low, pick, preferred_element_type=F32)
    )
    tile = jnp.concatenate([tile[6:80], jnp.zeros((14, 128), F32)], axis=0)
    lane = lax.broadcasted_iota(jnp.int32, (24, 128), 1)
    row = lax.broadcasted_iota(jnp.int32, (24, 128), 0)
    third = (lane >= GROUP).astype(jnp.int32) + (lane >= 2 * GROUP).astype(jnp.int32)
    taps = []
    for a in range(3):
        packed = jnp.where(
            third == 0, tile[a:a + 24], jnp.where(third == 1, tile[24 + a:48 + a], tile[48 + a:72 + a]))
        for b in range(3):
            taps.append(packed if b == 0 else pltpu.roll(packed, 128 - b, 1))
    image_row = bi * ROWS - 1 + row + 24 * third
    image_col = start - 1 + lane - GROUP * third
    valid = (image_row >= 0) & (image_row < nb * ROWS) & (image_col >= 0) & (image_col < WIDTH)
    channels = bias_ref.shape[0]
    spreads = []
    for part_of in range(3):
        rows = slice(8 * part_of, 8 * part_of + 8)
        mine = [tap[rows] for tap in taps]

        def channel(c, sums):
            value = mine[0] * fin_ref[0, 0, c] + bias_ref[c]
            for t in range(1, 9):
                value += mine[t] * fin_ref[t // 3, t % 3, c]
            value = jnp.maximum(value, 0.0)
            return tuple(sums[t] + value * fout_ref[t // 3, t % 3, c] for t in range(9))

        sums = lax.fori_loop(
            0, channels, channel, tuple(jnp.zeros((8, 128), F32) for t in range(9)), unroll=unroll)
        spreads.append(sums)
    mixed = jnp.zeros((ROWS, 128), F32)
    for t in range(9):
        a, b = t // 3, t % 3
        whole = jnp.where(valid, jnp.concatenate([s[t] for s in spreads], axis=0), 0.0)
        column = jnp.concatenate(
            [pltpu.roll(whole, (128 - GROUP * g - b) % 128, 1) for g in range(3)], axis=0)
        mixed += column[a:a + ROWS]
    centre = pltpu.roll(tile[2:2 + ROWS], 126, 1)
    den_ref[...] = (centre - mixed).T[:columns]

    bands(lambda b: sb(b, b).wait_recv())
    new = scb[0, 0:1]
    for b in range(1, nb):
        new += scb[b, 0:1]
    new = jnp.sum(new, axis=1, keepdims=True)
    dn_ref[...] = rn_ref[...] + (new / old) * dir_ref[...]

    def end_far(c):
        rs_up(c).wait_send()
        rs_down(c).wait_send()
    loop(0, half_nc, end_far)
    peers(lambda j: rs(j).wait_send())
    for copy in edges:
        copy.wait_send()
    peers(lambda j: to_peer(j).wait_send())
    loop(0, nc, lambda j: to_far(j).wait_send())
    peers(lambda j: rt(j, ci).wait_send())
    bands(lambda b: sa(b, bi).wait_send())
    peers(lambda j: gather(j, ci).wait_send())
    bands(lambda b: sb(b, bi).wait_send())


def place(*refs):
    count = len(refs) // 2
    sources, targets, sems = refs[:count], refs[count:2 * count], refs[-1]
    copies = [
        pltpu.make_async_copy(source, target, sems.at[i])
        for i, (source, target) in enumerate(zip(sources, targets))
    ]
    for copy in copies:
        copy.start()
    for copy in copies:
        copy.wait()


def per_device(nc, nb, unroll, estimate, residual, direction, kernels, weight_maps, filters_in, biases, filters_out):
    comps = weight_maps.shape[0]
    columns = WIDTH // nc
    vmem = pl.BlockSpec(memory_space=pltpu.VMEM)
    smem = pl.BlockSpec(memory_space=pltpu.SMEM)
    anywhere = pl.BlockSpec(memory_space=pl.ANY)
    band = jax.ShapeDtypeStruct((ROWS, WIDTH), F32)
    shapes = (band, band, band, jax.ShapeDtypeStruct((columns, ROWS), F32))
    dma = pltpu.SemaphoreType.DMA
    results = pl.pallas_call(
        functools.partial(kernel, nc, nb, unroll),
        out_shape=shapes,
        in_specs=[vmem] * 5 + [smem] * 3,
        out_specs=(vmem,) * 4,
        scratch_shapes=[
            pltpu.VMEM((2, 2, 8, WIDTH), F32),
            pltpu.VMEM((2, 2, 8, WIDTH), F32),
            pltpu.VMEM((comps, 128, 128), F32),
            pltpu.VMEM((comps, 128, 128), F32),
            pltpu.VMEM((comps, 128, 128), F32),
            pltpu.VMEM((2, 2, COARSE * ROWS, FINE * comps * ROWS), BF16),
            pltpu.VMEM((2, ROWS, comps * ROWS), BF16),
            pltpu.VMEM((2, comps, COARSE * ROWS, FINE * 128), BF16),
            pltpu.VMEM((comps, ROWS, 128), BF16),
            pltpu.VMEM((1 + 2 * FINE, comps * ROWS, WIDTH), BF16),
            pltpu.VMEM((1 + 2 * FINE, 128, WIDTH), BF16),
            pltpu.VMEM((COARSE * ROWS, WIDTH), F32),
            pltpu.VMEM((16, 8, WIDTH), F32),
            pltpu.VMEM((2 * nc, 8, WIDTH), F32),
            pltpu.VMEM((8, WIDTH), F32),
            pltpu.VMEM((16, 8, WIDTH), F32),
            pltpu.VMEM((8, 8, WIDTH), F32),
            pltpu.VMEM((8, 8, WIDTH), F32),
            pltpu.VMEM((8, 128), F32),
            pltpu.VMEM((nb, 8, 128), F32),
            pltpu.VMEM((nc, 3, 8, 128), F32),
            pltpu.VMEM((nb + 1, 8, 128), F32),
            pltpu.VMEM((80, WIDTH), F32),
            dma((2,)), dma((2,)),
            dma((16,)), dma((2 * nc,)),
            dma((nc,)), dma((nc,)), dma((16,)),
            dma((nc,)), dma((nc,)),
            dma((nb,)), dma((nb,)),
            dma((nc,)), dma((nc,)),
            dma((nb,)), dma((nb,)),
        ],
        compiler_params=pltpu.CompilerParams(
            collective_id=0, has_side_effects=True, vmem_limit_bytes=48 * 1024 * 1024),
        cost_estimate=pl.CostEstimate(
            flops=4 * 65 * comps * 64 * 128 * 256, bytes_accessed=1 << 20, transcendentals=0),
    )(estimate, residual, direction, kernels, weight_maps,
      filters_in.transpose(1, 2, 0), biases, filters_out.transpose(1, 2, 0))
    estimate_next, residual_next, direction_next, turned = pl.pallas_call(
        place,
        out_shape=shapes,
        in_specs=[vmem] * 4,
        out_specs=(anywhere,) * 4,
        scratch_shapes=[dma((4,))],
        compiler_params=pltpu.CompilerParams(vmem_limit_bytes=4 * 1024 * 1024),
    )(*results)
    return estimate_next, residual_next, direction_next, turned.T


def solution(mesh):
    nc, nb = mesh.shape["comp"], mesh.shape["band"]
    return jax.shard_map(
        functools.partial(per_device, nc, nb, 4),
        mesh=mesh,
        in_specs=(
            P("band", None),
            P("band", None),
            P("band", None),
            P("comp", None, None),
            P("comp", "band", None),
            P(),
            P(),
            P(),
        ),
        out_specs=(P("band", None), P("band", None), P("band", None), P("band", "comp")),
        check_vma=False,
    )
```

time: 50.8 us -> 44.2 us (0.87)
  Pallas kernels: 44.6 us -> 39.7 us
  local copies, waits for them, and re-layouts: 5.26 us -> 3.49 us
    pallas_call x1 -> x2, Pallas kernels: 44.6 us -> 39.7 us  [the longest x1 39 us: per_device(): pl.pallas_call(functools.partial(kernel, nc, nb, unroll), out_shape=shape...]
    pallas_call x1 -> x0, local copies, waits for them, and re-layouts: 0.68 us -> none  [per_device(): pl.pallas_call(functools.partial(kernel, nc, nb, unroll), out_shape=(band...]
    unnamed x20 -> x15, local copies, waits for them, and re-layouts: 4.16 us -> 3.49 us
where the time goes in v2:
time: 44.2 us; the launch traced here: 43.9 us
  Pallas kernels  39.7 us (90%)
  local copies, waits for them, and re-layouts  3.49 us (8%)
  between operations  0.72 us (2%)
    pallas_call x1, Pallas kernels, per_device(): pl.pallas_call(functools.partial(kernel, nc, nb, unroll), out_shape=shape...  39 us
    unnamed x15, local copies, waits for them, and re-layouts  3.49 us

profile of v2, /device:TPU:1, one launch (start us, length us, event | category | flops | bytes accessed | tf_op | source)
XLA Modules:
  0.0 43.9 jit_solution(4263557546074471565)
XLA Ops:
  0.6 0.0 copy-start
  0.6 0.0 copy-start.4
  0.7 0.0 copy-start.5
  0.7 0.0 copy-start.6
  0.7 1.0 %copy.12.ker_ref = bf16[4,65,65]{2,1,0:T(8,128)(2,1)S(1)} copy(bf16[4,65,65]{2,0,1:T(4,128)(2,1)} %param.11) | data formatting | bytes 67600 | tf_op args[3]
  1.6 0.0 copy-done
  1.6 0.0 copy-done.4
  1.7 0.0 copy-done.5
  1.7 0.0 copy-done.6
  1.7 0.0 copy-start.1
  1.7 0.8 %copy-done.1 = f32[64,256]{1,0:T(8,128)S(1)} copy-done((f32[64,256]{1,0:T(8,128)S(1)}, f32[64,256]{1,0:T(8,128)}, u32[]{:S(2)}) %copy-start.1) | copy-done | bytes 65560
  2.5 0.0 copy-start.2
  2.5 0.8 %copy-done.2 = f32[64,256]{1,0:T(8,128)S(1)} copy-done((f32[64,256]{1,0:T(8,128)S(1)}, f32[64,256]{1,0:T(8,128)}, u32[]{:S(2)}) %copy-start.2) | copy-done | bytes 65560
  3.4 0.0 copy-start.3
  3.4 0.8 %copy-done.3 = f32[64,256]{1,0:T(8,128)S(1)} copy-done((f32[64,256]{1,0:T(8,128)S(1)}, f32[64,256]{1,0:T(8,128)}, u32[]{:S(2)}) %copy-start.3) | copy-done | bytes 65560
  4.2 39.0 %shard_map.111 = (f32[64,256]{1,0:T(8,128)S(1)}, f32[64,256]{1,0:T(8,128)S(1)}, f32[64,256]{1,0:T(8,128)S(1)}, f32[32,64]{1,0:T(8,128)S(1)}) custom-call(f32[64,256]{1,0:T(8,128)S(1)} %copy-done.1, f32[64,256]{1,0:T(8,128)S(1)} %copy-done.2, f32[64,256]{1,0:T(8,128)S(1)} %copy-done.3, bf16[4,65,65]{2,1,0:T(8,128)(2,1)S(1)} %copy.12.ker_ref, ...), custom_call_target="tpu_custom_call" | custom-call | flops 2181038080 | bytes 1048576 | tf_op jit(solution)/shard_map/pallas_call | solution.py:409
  43.2 0.7 %shard_map.112 = (f32[64,256]{1,0:T(8,128)}, f32[64,256]{1,0:T(8,128)}, f32[64,256]{1,0:T(8,128)}, f32[32,64]{1,0:T(8,128)}) custom-call(f32[64,256]{1,0:T(8,128)S(1)} %get-tuple-element.12.refs_0_, f32[64,256]{1,0:T(8,128)S(1)} %get-tuple-element.13.refs_1_, f32[64,256]{1,0:T(8,128)S(1)} %get-tuple-element.14.refs_2_, f32[32,64]{1,0:T(8,128)S(1)} %get-tuple-element.15.refs_3_), custom_call_target="tpu_custom_call" | custom-call | tf_op jit(solution)/shard_map/pallas_call | solution.py:452
Async XLA Ops:
  0.6 1.0 %copy-start = (bf16[4,64,256]{2,1,0:T(8,128)(2,1)S(1)}, bf16[4,64,256]{2,1,0:T(8,128)(2,1)}, u32[]{:S(2)}) copy-start(bf16[4,64,256]{2,1,0:T(8,128)(2,1)} %w_ref.1) | copy-start | bytes 393220
  0.6 1.0 %copy-start.4 = (f32[64,3,3]{0,2,1:T(4,128)S(1)}, f32[64,3,3]{0,2,1:T(4,128)}, u32[]{:S(2)}) copy-start(f32[64,3,3]{0,2,1:T(4,128)} %param.13) | copy-start | bytes 6916
  0.7 1.0 %copy-start.5 = (f32[64,3,3]{0,2,1:T(4,128)S(1)}, f32[64,3,3]{0,2,1:T(4,128)}, u32[]{:S(2)}) copy-start(f32[64,3,3]{0,2,1:T(4,128)} %param.15) | copy-start | bytes 6916
  0.7 1.0 %copy-start.6 = (f32[64]{0:T(128)S(1)}, f32[64]{0:T(128)}, u32[]{:S(2)}) copy-start(f32[64]{0:T(128)} %bias_ref.1) | copy-start | bytes 772
  1.7 0.8 %copy-start.1 = (f32[64,256]{1,0:T(8,128)S(1)}, f32[64,256]{1,0:T(8,128)}, u32[]{:S(2)}) copy-start(f32[64,256]{1,0:T(8,128)} %est_ref.1) | copy-start | bytes 196612
  2.5 0.8 %copy-start.2 = (f32[64,256]{1,0:T(8,128)S(1)}, f32[64,256]{1,0:T(8,128)}, u32[]{:S(2)}) copy-start(f32[64,256]{1,0:T(8,128)} %res_ref.1) | copy-start | bytes 196612
  3.4 0.8 %copy-start.3 = (f32[64,256]{1,0:T(8,128)S(1)}, f32[64,256]{1,0:T(8,128)}, u32[]{:S(2)}) copy-start(f32[64,256]{1,0:T(8,128)} %dir_ref.1) | copy-start | bytes 196612

commit v3 on v2

--- a/solution.py
+++ b/solution.py
@@ -57,8 +57,9 @@
 
 def kernel(
     nc, nb, unroll,
-    est_ref, res_ref, dir_ref, ker_ref, w_ref, fin_ref, bias_ref, fout_ref,
+    est_hbm, res_hbm, dir_hbm, ker_hbm, w_hbm, fin_hbm, bias_hbm, fout_hbm,
     en_ref, rn_ref, dn_ref, den_ref,
+    est_ref, res_ref, dir_ref, ker_ref, w_ref, fin_ref, bias_ref, fout_ref, fetch_s,
     edge, edge_halo, kscr, kt, ktj, gf, gz, hb, hz, shifted, ishift, acc,
     part, rsbuf, iblk, iwin, part2, rsbuf2, sca, sca_in, ag, scb, ext,
     h_s, h_r, rs_s, rs_r, iw_s, in_s, iw_r, rt_s, rt_r, sa_s, sa_r, ag_s, ag_r, sb_s, sb_r,
@@ -76,6 +77,16 @@
     def bands(fn):
         loop(1, nb, lambda d: fn(lax.rem(bi + d, nb)))
 
+    fetches = [
+        pltpu.make_async_copy(source, target, fetch_s.at[i])
+        for i, (source, target) in enumerate((
+            (ker_hbm, ker_ref), (dir_hbm, dir_ref), (w_hbm, w_ref), (res_hbm, res_ref),
+            (est_hbm, est_ref), (fin_hbm, fin_ref), (bias_hbm, bias_ref), (fout_hbm, fout_ref)))
+    ]
+    for copy in fetches:
+        copy.start()
+    ends = []
+
     barrier = pltpu.get_barrier_semaphore()
 
     def greet(comp, band):
@@ -88,32 +99,26 @@
     peers(lambda j: greet(j, bi))
     loop(2, nb - 1, lambda d: greet(ci, lax.rem(bi + d, nb)))
 
+    size = 128
+    kscr[...] = jnp.zeros_like(kscr)
+    anti_r = lax.broadcasted_iota(jnp.int32, (size, size), 0)
+    anti_c = lax.broadcasted_iota(jnp.int32, (size, size), 1)
+    anti = (anti_r + anti_c == SPAN - 1).astype(BF16)
+    fetches[0].wait()
+    for a in range(SPAN):
+        kscr[:, a, 0:SPAN] = ker_ref[a].astype(F32)
+    for k in range(comps):
+        turned = kscr[k].T
+        kt[k] = turned
+        ktj[k] = jnp.dot(turned.astype(BF16), anti, preferred_element_type=F32)
+
+    fetches[1].wait()
+    fetches[2].wait()
     direction = dir_ref[...]
     for k in range(comps):
         shaped = (w_ref[k].astype(F32) * direction).astype(BF16)
         for at, value in all_shifts(shaped):
             shifted[at, pl.ds(k * ROWS, ROWS), :] = value
-    edge[0, 0] = est_ref[:8]
-    edge[0, 1] = dir_ref[:8]
-    edge[1, 0] = est_ref[ROWS - 8:]
-    edge[1, 1] = dir_ref[ROWS - 8:]
-    residual = res_ref[...]
-    sca[...] = jnp.zeros_like(sca)
-    sca[1:2] = fold(direction * direction)
-    sca[2:3] = fold(residual * residual)
-
-    size = 128
-    kscr[...] = jnp.zeros_like(kscr)
-    anti_r = lax.broadcasted_iota(jnp.int32, (size, size), 0)
-    anti_c = lax.broadcasted_iota(jnp.int32, (size, size), 1)
-    anti = (anti_r + anti_c == SPAN - 1).astype(BF16)
-    for k in range(comps):
-        kscr[k, 0:SPAN, 0:SPAN] = ker_ref[k].astype(F32)
-    for k in range(comps):
-        turned = kscr[k].T
-        kt[k] = turned
-        ktj[k] = jnp.dot(turned.astype(BF16), anti, preferred_element_type=F32)
-
     def band_matrix(table, k, b, first=0):
         row = table[k, pl.ds(b, 1), :]
         spread = jnp.broadcast_to(row, (ROWS, 128))
@@ -160,6 +165,16 @@
         for q in range(8):
             part[base + q] = total[8 * q:8 * q + 8]
 
+    for copy in fetches[3:]:
+        copy.wait()
+    edge[0, 0] = est_ref[:8]
+    edge[0, 1] = dir_ref[:8]
+    edge[1, 0] = est_ref[ROWS - 8:]
+    edge[1, 1] = dir_ref[ROWS - 8:]
+    residual = res_ref[...]
+    sca[...] = jnp.zeros_like(sca)
+    sca[1:2] = fold(direction * direction)
+    sca[2:3] = fold(residual * residual)
     pl.semaphore_wait(barrier, nc - 1 + 2 * nc + nb - 3)
 
     def rs_up(c):
@@ -186,6 +201,13 @@
     ]
     for copy in edges:
         copy.start()
+
+    def end_far(c):
+        rs_up(c).wait_send()
+        rs_down(c).wait_send()
+    ends.append(lambda: loop(0, half_nc, end_far))
+    ends.append(lambda: peers(lambda j: rs(j).wait_send()))
+    ends.extend(copy.wait_send for copy in edges)
 
     def build_back(s1):
         at = pl.ds(pl.multiple_of(s1 * ROWS, ROWS), ROWS)
@@ -221,6 +243,8 @@
         return remote(iblk, iwin.at[far_slot], in_s.at[j], iw_r.at[far_slot], j, far_band)
     loop(0, nc, lambda j: to_far(j).start())
     peers(lambda j: to_peer(j).start())
+    ends.append(lambda: peers(lambda j: to_peer(j).wait_send()))
+    ends.append(lambda: loop(0, nc, lambda j: to_far(j).wait_send()))
 
     def window(at):
         return remote(iblk, iwin.at[at], iw_s.at[0], iw_r.at[at], ci, up)
@@ -256,11 +280,13 @@
     def rt(j, slot):
         return remote(part2.at[j], rsbuf2.at[slot], rt_s.at[j], rt_r.at[slot], j, bi)
     peers(lambda j: rt(j, ci).start())
+    ends.append(lambda: peers(lambda j: rt(j, ci).wait_send()))
     sca[0:1] = fold(dir_ref[...] * rsum)
 
     def sa(b, slot):
         return remote(sca, sca_in.at[slot], sa_s.at[b], sa_r.at[slot], ci, b)
     bands(lambda b: sa(b, bi).start())
+    ends.append(lambda: bands(lambda b: sa(b, bi).wait_send()))
     sca_in[bi] = sca[...]
     rsbuf2[ci] = part2[ci]
 
@@ -279,6 +305,7 @@
     def gather(j, slot):
         return remote(ag.at[ci], ag.at[slot], ag_s.at[j], ag_r.at[slot], j, bi)
     peers(lambda j: gather(j, ci).start())
+    ends.append(lambda: peers(lambda j: gather(j, ci).wait_send()))
     peers(lambda j: gather(j, j).wait_recv())
 
     product = ag[0, 2, 0:1]
@@ -298,6 +325,7 @@
     def sb(b, slot):
         return remote(scb.at[nb], scb.at[slot], sb_s.at[b], sb_r.at[slot], ci, b)
     bands(lambda b: sb(b, bi).start())
+    ends.append(lambda: bands(lambda b: sb(b, bi).wait_send()))
     scb[bi] = scb[nb]
     for copy in edges:
         copy.wait_recv()
@@ -369,19 +397,8 @@
     new = jnp.sum(new, axis=1, keepdims=True)
     dn_ref[...] = rn_ref[...] + (new / old) * dir_ref[...]
 
-    def end_far(c):
-        rs_up(c).wait_send()
-        rs_down(c).wait_send()
-    loop(0, half_nc, end_far)
-    peers(lambda j: rs(j).wait_send())
-    for copy in edges:
-        copy.wait_send()
-    peers(lambda j: to_peer(j).wait_send())
-    loop(0, nc, lambda j: to_far(j).wait_send())
-    peers(lambda j: rt(j, ci).wait_send())
-    bands(lambda b: sa(b, bi).wait_send())
-    peers(lambda j: gather(j, ci).wait_send())
-    bands(lambda b: sb(b, bi).wait_send())
+    for end in ends:
+        end()
 
 
 def place(*refs):
@@ -401,7 +418,7 @@
     comps = weight_maps.shape[0]
     columns = WIDTH // nc
     vmem = pl.BlockSpec(memory_space=pltpu.VMEM)
-    smem = pl.BlockSpec(memory_space=pltpu.SMEM)
+    hbm = pl.BlockSpec(memory_space=pltpu.HBM)
     anywhere = pl.BlockSpec(memory_space=pl.ANY)
     band = jax.ShapeDtypeStruct((ROWS, WIDTH), F32)
     shapes = (band, band, band, jax.ShapeDtypeStruct((columns, ROWS), F32))
@@ -409,9 +426,18 @@
     results = pl.pallas_call(
         functools.partial(kernel, nc, nb, unroll),
         out_shape=shapes,
-        in_specs=[vmem] * 5 + [smem] * 3,
+        in_specs=[hbm] * 8,
         out_specs=(vmem,) * 4,
         scratch_shapes=[
+            pltpu.VMEM((ROWS, WIDTH), F32),
+            pltpu.VMEM((ROWS, WIDTH), F32),
+            pltpu.VMEM((ROWS, WIDTH), F32),
+            pltpu.VMEM((SPAN, comps, SPAN), BF16),
+            pltpu.VMEM((comps, ROWS, WIDTH), BF16),
+            pltpu.SMEM((3, 3, filters_in.shape[0]), F32),
+            pltpu.SMEM(biases.shape, F32),
+            pltpu.SMEM((3, 3, filters_in.shape[0]), F32),
+            dma((8,)),
             pltpu.VMEM((2, 2, 8, WIDTH), F32),
             pltpu.VMEM((2, 2, 8, WIDTH), F32),
             pltpu.VMEM((comps, 128, 128), F32),
@@ -444,10 +470,10 @@
             dma((nb,)), dma((nb,)),
         ],
         compiler_params=pltpu.CompilerParams(
-            collective_id=0, has_side_effects=True, vmem_limit_bytes=48 * 1024 * 1024),
+            collective_id=0, has_side_effects=True, vmem_limit_bytes=54960 * 1024),
         cost_estimate=pl.CostEstimate(
             flops=4 * 65 * comps * 64 * 128 * 256, bytes_accessed=1 << 20, transcendentals=0),
-    )(estimate, residual, direction, kernels, weight_maps,
+    )(estimate, residual, direction, kernels.transpose(1, 0, 2), weight_maps,
       filters_in.transpose(1, 2, 0), biases, filters_out.transpose(1, 2, 0))
     estimate_next, residual_next, direction_next, turned = pl.pallas_call(
         place,

time: 44.2 us -> 41.9 us (0.948)
  local copies, waits for them, and re-layouts: 3.49 us -> 2.03 us
  Pallas kernels: 39.7 us -> 39 us
    unnamed x15 -> x6, local copies, waits for them, and re-layouts: 3.49 us -> 2.03 us
    pallas_call x1, Pallas kernels: 39 us -> 38.3 us  [per_device(): pl.pallas_call(functools.partial(kernel, nc, nb, unroll), out_shape=shape...]
where the time goes in v3:
time: 41.9 us; the launch traced here: 41.7 us
  Pallas kernels  39 us (93%)
  local copies, waits for them, and re-layouts  2.03 us (5%)
  between operations  0.65 us (2%)
    pallas_call x1, Pallas kernels, per_device(): pl.pallas_call(functools.partial(kernel, nc, nb, unroll), out_shape=shape...  38.3 us
    unnamed x6, local copies, waits for them, and re-layouts  2.03 us

profile of v3, /device:TPU:1, one launch (start us, length us, event | category | flops | bytes accessed | tf_op | source)
XLA Modules:
  0.0 41.7 jit_solution(17695561218116085172)
XLA Ops:
  0.6 0.0 copy-start.2
  0.6 0.6 %copy-done.2 = f32[64]{0:T(128)S(1)} copy-done((f32[64]{0:T(128)S(1)}, f32[64]{0:T(128)}, u32[]{:S(2)}) %copy-start.2) | copy-done | bytes 280
  1.3 0.0 copy-start
  1.3 0.7 %copy-done = f32[64,3,3]{0,2,1:T(4,128)S(1)} copy-done((f32[64,3,3]{0,2,1:T(4,128)S(1)}, f32[64,3,3]{0,2,1:T(4,128)}, u32[]{:S(2)}) %copy-start) | copy-done | bytes 2328
  2.0 0.0 copy-start.1
  2.0 0.7 %copy-done.1 = f32[64,3,3]{0,2,1:T(4,128)S(1)} copy-done((f32[64,3,3]{0,2,1:T(4,128)S(1)}, f32[64,3,3]{0,2,1:T(4,128)}, u32[]{:S(2)}) %copy-start.1) | copy-done | bytes 2328
  2.7 38.3 %shard_map.111 = (f32[64,256]{1,0:T(8,128)S(1)}, f32[64,256]{1,0:T(8,128)S(1)}, f32[64,256]{1,0:T(8,128)S(1)}, f32[32,64]{1,0:T(8,128)S(1)}) custom-call(f32[64,256]{1,0:T(8,128)} %est_hbm.1, f32[64,256]{1,0:T(8,128)} %res_hbm.1, f32[64,256]{1,0:T(8,128)} %dir_hbm.1, bf16[65,4,65]{2,1,0:T(4,128)(2,1)} %bitcast.6, bf16[4,64,256]{2,1,0:T(8,128)(2,1)} %w_hbm.1, ...), custom_call_target="tpu_custom_call" | custom-call | flops 2181038080 | bytes 1048576 | tf_op jit(solution)/shard_map/pallas_call | solution.py:426
  41.0 0.7 %shard_map.112 = (f32[64,256]{1,0:T(8,128)}, f32[64,256]{1,0:T(8,128)}, f32[64,256]{1,0:T(8,128)}, f32[32,64]{1,0:T(8,128)}) custom-call(f32[64,256]{1,0:T(8,128)S(1)} %get-tuple-element.12.refs_0_, f32[64,256]{1,0:T(8,128)S(1)} %get-tuple-element.13.refs_1_, f32[64,256]{1,0:T(8,128)S(1)} %get-tuple-element.14.refs_2_, f32[32,64]{1,0:T(8,128)S(1)} %get-tuple-element.15.refs_3_), custom_call_target="tpu_custom_call" | custom-call | tf_op jit(solution)/shard_map/pallas_call | solution.py:478
Async XLA Ops:
  0.6 0.7 %copy-start.2 = (f32[64]{0:T(128)S(1)}, f32[64]{0:T(128)}, u32[]{:S(2)}) copy-start(f32[64]{0:T(128)} %bias_hbm.1) | copy-start | bytes 772
  1.3 0.7 %copy-start = (f32[64,3,3]{0,2,1:T(4,128)S(1)}, f32[64,3,3]{0,2,1:T(4,128)}, u32[]{:S(2)}) copy-start(f32[64,3,3]{0,2,1:T(4,128)} %param.13) | copy-start | bytes 6916
  2.0 0.7 %copy-start.1 = (f32[64,3,3]{0,2,1:T(4,128)S(1)}, f32[64,3,3]{0,2,1:T(4,128)}, u32[]{:S(2)}) copy-start(f32[64,3,3]{0,2,1:T(4,128)} %param.15) | copy-start | bytes 6916

commit v4 on v3

--- a/solution.py
+++ b/solution.py
@@ -470,11 +470,12 @@
             dma((nb,)), dma((nb,)),
         ],
         compiler_params=pltpu.CompilerParams(
-            collective_id=0, has_side_effects=True, vmem_limit_bytes=54960 * 1024),
+            collective_id=0, has_side_effects=True, vmem_limit_bytes=48 * 1024 * 1024),
         cost_estimate=pl.CostEstimate(
             flops=4 * 65 * comps * 64 * 128 * 256, bytes_accessed=1 << 20, transcendentals=0),
-    )(estimate, residual, direction, kernels.transpose(1, 0, 2), weight_maps,
-      filters_in.transpose(1, 2, 0), biases, filters_out.transpose(1, 2, 0))
+    )(*(pltpu.with_memory_space_constraint(x, pltpu.HBM) for x in (
+        estimate, residual, direction, kernels.transpose(1, 0, 2), weight_maps,
+        filters_in.transpose(1, 2, 0), biases, filters_out.transpose(1, 2, 0))))
     estimate_next, residual_next, direction_next, turned = pl.pallas_call(
         place,
         out_shape=shapes,

time: 41.9 us -> 39.9 us (0.952)
  local copies, waits for them, and re-layouts: 2.03 us -> 0 us
    unnamed x6 -> x0, local copies, waits for them, and re-layouts: 2.03 us -> none
where the time goes in v4:
time: 39.9 us; the launch traced here: 39.8 us
  Pallas kernels  39.1 us (98%)
  between operations  0.64 us (2%)
    pallas_call x1, Pallas kernels, per_device(): pl.pallas_call(functools.partial(kernel, nc, nb, unroll), out_shape=shape...  38.4 us

profile of v4, /device:TPU:1, one launch (start us, length us, event | category | flops | bytes accessed | tf_op | source)
XLA Modules:
  0.0 39.8 jit_solution(3224662071876945058)
XLA Ops:
  0.6 38.4 %shard_map.111 = (f32[64,256]{1,0:T(8,128)S(1)}, f32[64,256]{1,0:T(8,128)S(1)}, f32[64,256]{1,0:T(8,128)S(1)}, f32[32,64]{1,0:T(8,128)S(1)}) custom-call(f32[64,256]{1,0:T(8,128)} %est_hbm.1, f32[64,256]{1,0:T(8,128)} %res_hbm.1, f32[64,256]{1,0:T(8,128)} %dir_hbm.1, bf16[65,4,65]{2,1,0:T(4,128)(2,1)} %bitcast.4, bf16[4,64,256]{2,1,0:T(8,128)(2,1)} %w_hbm.1, ...), custom_call_target="tpu_custom_call" | custom-call | flops 2181038080 | bytes 1048576 | tf_op jit(solution)/shard_map/pallas_call | solution.py:426
  39.0 0.7 %shard_map.112 = (f32[64,256]{1,0:T(8,128)}, f32[64,256]{1,0:T(8,128)}, f32[64,256]{1,0:T(8,128)}, f32[32,64]{1,0:T(8,128)}) custom-call(f32[64,256]{1,0:T(8,128)S(1)} %get-tuple-element.12.refs_0_, f32[64,256]{1,0:T(8,128)S(1)} %get-tuple-element.13.refs_1_, f32[64,256]{1,0:T(8,128)S(1)} %get-tuple-element.14.refs_2_, f32[32,64]{1,0:T(8,128)S(1)} %get-tuple-element.15.refs_3_), custom_call_target="tpu_custom_call" | custom-call | tf_op jit(solution)/shard_map/pallas_call | solution.py:479

commit v5 on v4

--- a/solution.py
+++ b/solution.py
@@ -15,8 +15,10 @@
 SPAN = 65
 ROWS = 64
 WIDTH = 256
-FINE = 8
-COARSE = 4
+FINE = 4
+COARSE = 8
+BACK_FINE = 8
+BACK_COARSE = 4
 GROUP = 40
 
 
@@ -36,9 +38,19 @@
 
 def all_shifts(x):
     yield 0, x
-    for s0 in range(FINE):
+    for s0 in range(BACK_FINE):
         yield 1 + s0, lane_shift(x, 1 + s0)
-        yield 1 + FINE + s0, lane_shift(x, -1 - s0)
+        yield 1 + BACK_FINE + s0, lane_shift(x, -1 - s0)
+
+
+def swap_pairs(x):
+    return jnp.concatenate(
+        [x[(k ^ 1) * ROWS:(k ^ 1) * ROWS + ROWS] for k in range(x.shape[0] // ROWS)], axis=0)
+
+
+def far_first(fns):
+    for hops, fn in sorted(fns, key=lambda pair: -pair[0]):
+        fn()
 
 
 def loop(low, high, fn):
@@ -60,7 +72,7 @@
     est_hbm, res_hbm, dir_hbm, ker_hbm, w_hbm, fin_hbm, bias_hbm, fout_hbm,
     en_ref, rn_ref, dn_ref, den_ref,
     est_ref, res_ref, dir_ref, ker_ref, w_ref, fin_ref, bias_ref, fout_ref, fetch_s,
-    edge, edge_halo, kscr, kt, ktj, gf, gz, hb, hz, shifted, ishift, acc,
+    edge, edge_halo, kscr, kt, ktj, facc, shaped, hb, hz, ishift, acc,
     part, rsbuf, iblk, iwin, part2, rsbuf2, sca, sca_in, ag, scb, ext,
     h_s, h_r, rs_s, rs_r, iw_s, in_s, iw_r, rt_s, rt_r, sa_s, sa_r, ag_s, ag_r, sb_s, sb_r,
 ):
@@ -77,6 +89,32 @@
     def bands(fn):
         loop(1, nb, lambda d: fn(lax.rem(bi + d, nb)))
 
+    def ring(d, n):
+        return min(d, n - d)
+
+    xs = nc // 2
+    far_peers = [
+        (ring(dx, xs) + 2 * dz,
+         lax.rem(lax.div(ci, 2) + dx, xs) * 2 + lax.rem(ci + dz, 2))
+        for dx in range(xs) for dz in range(2) if dx or dz
+    ]
+    if nb % 4 == 0:
+        ys = nb // 4
+        far_bands = [
+            (ring(dy, ys) + dz + dc / 2,
+             lax.rem(lax.div(bi, 2 * ys) + dz, 2) * 2 * ys
+             + lax.rem(lax.rem(lax.div(bi, 2), ys) + dy, ys) * 2 + lax.rem(bi + dc, 2))
+            for dz in range(2) for dy in range(ys) for dc in range(2) if dz or dy or dc
+        ]
+    else:
+        far_bands = [(1, lax.rem(bi + d, nb)) for d in range(1, nb)]
+
+    def to_peers(fn):
+        return [(hops, lambda j=j: fn(j)) for hops, j in far_peers]
+
+    def to_bands(fn):
+        return [(hops, lambda b=b: fn(b)) for hops, b in far_bands]
+
     fetches = [
         pltpu.make_async_copy(source, target, fetch_s.at[i])
         for i, (source, target) in enumerate((
@@ -99,26 +137,19 @@
     peers(lambda j: greet(j, bi))
     loop(2, nb - 1, lambda d: greet(ci, lax.rem(bi + d, nb)))
 
-    size = 128
     kscr[...] = jnp.zeros_like(kscr)
-    anti_r = lax.broadcasted_iota(jnp.int32, (size, size), 0)
-    anti_c = lax.broadcasted_iota(jnp.int32, (size, size), 1)
-    anti = (anti_r + anti_c == SPAN - 1).astype(BF16)
     fetches[0].wait()
     for a in range(SPAN):
         kscr[:, a, 0:SPAN] = ker_ref[a].astype(F32)
     for k in range(comps):
-        turned = kscr[k].T
-        kt[k] = turned
-        ktj[k] = jnp.dot(turned.astype(BF16), anti, preferred_element_type=F32)
+        kt[k] = kscr[k].T
 
     fetches[1].wait()
     fetches[2].wait()
     direction = dir_ref[...]
     for k in range(comps):
-        shaped = (w_ref[k].astype(F32) * direction).astype(BF16)
-        for at, value in all_shifts(shaped):
-            shifted[at, pl.ds(k * ROWS, ROWS), :] = value
+        shaped[pl.ds(k * ROWS, ROWS), :] = (w_ref[k].astype(F32) * direction).astype(BF16)
+
     def band_matrix(table, k, b, first=0):
         row = table[k, pl.ds(b, 1), :]
         spread = jnp.broadcast_to(row, (ROWS, 128))
@@ -133,34 +164,32 @@
         upper = jnp.where(left, odd, even).astype(BF16)
         return lower, upper
 
-    def build_forward(s1):
-        at = pl.ds(pl.multiple_of(s1 * ROWS, ROWS), ROWS)
+    def forward_matrices(columns):
+        lower, upper = [], []
+        for b in columns:
+            pairs = [forward_pair(k, b) for k in range(0, comps, 2)]
+            lower.append(jnp.concatenate([pair[0] for pair in pairs], axis=1))
+            upper.append(jnp.concatenate([pair[1] for pair in pairs], axis=1))
+        return jnp.concatenate(lower, axis=0), jnp.concatenate(upper, axis=0)
+
+    for s0 in range(FINE):
         for side, sign in ((0, 1), (1, -1)):
-            for s0 in range(FINE):
-                b = HALF + sign * (1 + s0 + FINE * s1)
-                for k in range(0, comps, 2):
-                    lanes = pl.ds(s0 * comps * ROWS + k * ROWS, 128)
-                    gf[side, 0, at, lanes], gf[side, 1, at, lanes] = forward_pair(k, b)
-    loop(0, COARSE, build_forward)
-    for k in range(0, comps, 2):
-        gz[0, :, pl.ds(k * ROWS, 128)], gz[1, :, pl.ds(k * ROWS, 128)] = forward_pair(k, HALF)
-
-    depth = comps * ROWS
-
-    def taken(at, where):
-        if where == 0:
-            return shifted[at]
-        return jnp.concatenate(
-            [shifted[at, pl.ds((k ^ 1) * ROWS, ROWS), :] for k in range(comps)], axis=0)
-
-    for where in range(2):
-        total = jnp.dot(gz[where], taken(0, where), preferred_element_type=F32)
+            source = lane_shift(shaped[...], sign * (1 + s0))
+            lower, upper = forward_matrices(
+                [HALF + sign * (1 + s0 + FINE * s1) for s1 in range(COARSE)])
+            for where, matrix, rows in ((0, lower, source), (1, upper, swap_pairs(source))):
+                product = jnp.dot(matrix, rows, preferred_element_type=F32)
+                if s0 == 0:
+                    facc[side, where] = product
+                else:
+                    facc[side, where] += product
+    lower, upper = forward_matrices([HALF])
+    for where, matrix, rows in ((0, lower, shaped[...]), (1, upper, swap_pairs(shaped[...]))):
+        total = jnp.dot(matrix, rows, preferred_element_type=F32)
         for side, sign in ((0, 1), (1, -1)):
-            source = jnp.concatenate(
-                [taken(1 + side * FINE + s0, where) for s0 in range(FINE)], axis=0)
-            acc[...] = jnp.dot(gf[side, where], source, preferred_element_type=F32)
             for s1 in range(COARSE):
-                total += lane_shift(acc[pl.ds(s1 * ROWS, ROWS), :], sign * FINE * s1)
+                total += lane_shift(
+                    facc[side, where, pl.ds(s1 * ROWS, ROWS), :], sign * FINE * s1)
         base = 8 * (1 - where)
         for q in range(8):
             part[base + q] = total[8 * q:8 * q + 8]
@@ -194,7 +223,7 @@
         rs_up(c).start()
         rs_down(c).start()
     loop(0, half_nc, start_far)
-    peers(lambda j: rs(j).start())
+    far_first(to_peers(lambda j: rs(j).start()))
     edges = [
         remote(edge.at[0], edge_halo.at[1], h_s.at[0], h_r.at[1], ci, up),
         remote(edge.at[1], edge_halo.at[0], h_s.at[1], h_r.at[0], ci, down),
@@ -209,14 +238,21 @@
     ends.append(lambda: peers(lambda j: rs(j).wait_send()))
     ends.extend(copy.wait_send for copy in edges)
 
+    size = 128
+    anti_r = lax.broadcasted_iota(jnp.int32, (size, size), 0)
+    anti_c = lax.broadcasted_iota(jnp.int32, (size, size), 1)
+    anti = (anti_r + anti_c == SPAN - 1).astype(BF16)
+    for k in range(comps):
+        ktj[k] = jnp.dot(kt[k].astype(BF16), anti, preferred_element_type=F32)
+
     def build_back(s1):
         at = pl.ds(pl.multiple_of(s1 * ROWS, ROWS), ROWS)
         for side, sign in ((0, 1), (1, -1)):
-            for s0 in range(FINE):
-                b = HALF - sign * (1 + s0 + FINE * s1)
+            for s0 in range(BACK_FINE):
+                b = HALF - sign * (1 + s0 + BACK_FINE * s1)
                 for k in range(comps):
                     hb[side, k, at, pl.ds(s0 * 128, 128)] = band_matrix(ktj, k, b).astype(BF16)
-    loop(0, COARSE, build_back)
+    loop(0, BACK_COARSE, build_back)
     for k in range(comps):
         hz[k] = band_matrix(ktj, k, HALF).astype(BF16)
 
@@ -231,7 +267,7 @@
         away += rsbuf[nc + j]
     linked = ((bi > 0) | (far == 1)) & ((bi < nb - 1) | (far == 0))
     block = near + jnp.where(linked, away, 0.0)
-    iblk[...] = block.astype(BF16).astype(F32)
+    iblk[...] = jnp.concatenate([block[:, :128], block[:, 128:]], axis=0).astype(BF16)
     iwin[ci + 4] = iblk[...]
     far_band = lax.rem(bi + nb - 1 + 2 * far, nb)
     far_slot = ci + 12 - 16 * far
@@ -242,7 +278,7 @@
     def to_far(j):
         return remote(iblk, iwin.at[far_slot], in_s.at[j], iw_r.at[far_slot], j, far_band)
     loop(0, nc, lambda j: to_far(j).start())
-    peers(lambda j: to_peer(j).start())
+    far_first(to_peers(lambda j: to_peer(j).start()))
     ends.append(lambda: peers(lambda j: to_peer(j).wait_send()))
     ends.append(lambda: loop(0, nc, lambda j: to_far(j).wait_send()))
 
@@ -257,7 +293,10 @@
 
     inside = ((bi > 0).astype(F32), (bi < nb - 1).astype(F32))
     for r in range(0, 16, 2):
-        pair = jnp.concatenate([iwin[r], iwin[r + 1]], axis=0)
+        first, second = iwin[r].astype(F32), iwin[r + 1].astype(F32)
+        pair = jnp.concatenate([
+            jnp.concatenate([first[:8], first[8:]], axis=1),
+            jnp.concatenate([second[:8], second[8:]], axis=1)], axis=0)
         if r < 4:
             pair = pair * inside[0]
         if r >= 12:
@@ -269,23 +308,22 @@
     for k in range(comps):
         back = jnp.dot(hz[k], ishift[0], preferred_element_type=F32)
         for side, sign in ((0, 1), (1, -1)):
-            source = ishift[pl.ds(1 + side * FINE, FINE)].reshape(FINE * 128, WIDTH)
+            source = ishift[pl.ds(1 + side * BACK_FINE, BACK_FINE)].reshape(BACK_FINE * 128, WIDTH)
             acc[...] = jnp.dot(hb[side, k], source, preferred_element_type=F32)
-            for s1 in range(COARSE):
-                back += lane_shift(acc[pl.ds(s1 * ROWS, ROWS), :], sign * FINE * s1)
+            for s1 in range(BACK_COARSE):
+                back += lane_shift(acc[pl.ds(s1 * ROWS, ROWS), :], sign * BACK_FINE * s1)
         rsum += w_ref[k].astype(F32) * back
     for j in range(8):
         part2[j] = rsum[8 * j:8 * j + 8]
 
     def rt(j, slot):
         return remote(part2.at[j], rsbuf2.at[slot], rt_s.at[j], rt_r.at[slot], j, bi)
-    peers(lambda j: rt(j, ci).start())
     ends.append(lambda: peers(lambda j: rt(j, ci).wait_send()))
     sca[0:1] = fold(dir_ref[...] * rsum)
 
     def sa(b, slot):
         return remote(sca, sca_in.at[slot], sa_s.at[b], sa_r.at[slot], ci, b)
-    bands(lambda b: sa(b, bi).start())
+    far_first(to_peers(lambda j: rt(j, ci).start()) + to_bands(lambda b: sa(b, bi).start()))
     ends.append(lambda: bands(lambda b: sa(b, bi).wait_send()))
     sca_in[bi] = sca[...]
     rsbuf2[ci] = part2[ci]
@@ -304,7 +342,7 @@
 
     def gather(j, slot):
         return remote(ag.at[ci], ag.at[slot], ag_s.at[j], ag_r.at[slot], j, bi)
-    peers(lambda j: gather(j, ci).start())
+    far_first(to_peers(lambda j: gather(j, ci).start()))
     ends.append(lambda: peers(lambda j: gather(j, ci).wait_send()))
     peers(lambda j: gather(j, j).wait_recv())
 
@@ -324,7 +362,7 @@
 
     def sb(b, slot):
         return remote(scb.at[nb], scb.at[slot], sb_s.at[b], sb_r.at[slot], ci, b)
-    bands(lambda b: sb(b, bi).start())
+    far_first(to_bands(lambda b: sb(b, bi).start()))
     ends.append(lambda: bands(lambda b: sb(b, bi).wait_send()))
     scb[bi] = scb[nb]
     for copy in edges:
@@ -443,17 +481,16 @@
             pltpu.VMEM((comps, 128, 128), F32),
             pltpu.VMEM((comps, 128, 128), F32),
             pltpu.VMEM((comps, 128, 128), F32),
-            pltpu.VMEM((2, 2, COARSE * ROWS, FINE * comps * ROWS), BF16),
-            pltpu.VMEM((2, ROWS, comps * ROWS), BF16),
-            pltpu.VMEM((2, comps, COARSE * ROWS, FINE * 128), BF16),
+            pltpu.VMEM((2, 2, COARSE * ROWS, WIDTH), F32),
+            pltpu.VMEM((comps * ROWS, WIDTH), BF16),
+            pltpu.VMEM((2, comps, BACK_COARSE * ROWS, BACK_FINE * 128), BF16),
             pltpu.VMEM((comps, ROWS, 128), BF16),
-            pltpu.VMEM((1 + 2 * FINE, comps * ROWS, WIDTH), BF16),
-            pltpu.VMEM((1 + 2 * FINE, 128, WIDTH), BF16),
-            pltpu.VMEM((COARSE * ROWS, WIDTH), F32),
+            pltpu.VMEM((1 + 2 * BACK_FINE, 128, WIDTH), BF16),
+            pltpu.VMEM((BACK_COARSE * ROWS, WIDTH), F32),
             pltpu.VMEM((16, 8, WIDTH), F32),
             pltpu.VMEM((2 * nc, 8, WIDTH), F32),
-            pltpu.VMEM((8, WIDTH), F32),
-            pltpu.VMEM((16, 8, WIDTH), F32),
+            pltpu.VMEM((16, 128), BF16),
+            pltpu.VMEM((16, 16, 128), BF16),
             pltpu.VMEM((8, 8, WIDTH), F32),
             pltpu.VMEM((8, 8, WIDTH), F32),
             pltpu.VMEM((8, 128), F32),

time: 39.9 us -> 38.3 us (0.960)
  Pallas kernels: 39.1 us -> 37.4 us
    pallas_call x1, Pallas kernels: 38.4 us -> 36.7 us  [per_device(): pl.pallas_call(functools.partial(kernel, nc, nb, unroll), out_shape=shape...]
where the time goes in v5:
time: 38.3 us; the launch traced here: 38.1 us
  Pallas kernels  37.4 us (98%)
  between operations  0.64 us (2%)
    pallas_call x1, Pallas kernels, per_device(): pl.pallas_call(functools.partial(kernel, nc, nb, unroll), out_shape=shape...  36.7 us

profile of v5, /device:TPU:1, one launch (start us, length us, event | category | flops | bytes accessed | tf_op | source)
XLA Modules:
  0.0 38.1 jit_solution(16997671418323368222)
XLA Ops:
  0.6 36.7 %shard_map.111 = (f32[64,256]{1,0:T(8,128)S(1)}, f32[64,256]{1,0:T(8,128)S(1)}, f32[64,256]{1,0:T(8,128)S(1)}, f32[32,64]{1,0:T(8,128)S(1)}) custom-call(f32[64,256]{1,0:T(8,128)} %est_hbm.1, f32[64,256]{1,0:T(8,128)} %res_hbm.1, f32[64,256]{1,0:T(8,128)} %dir_hbm.1, bf16[65,4,65]{2,1,0:T(4,128)(2,1)} %bitcast.4, bf16[4,64,256]{2,1,0:T(8,128)(2,1)} %w_hbm.1, ...), custom_call_target="tpu_custom_call" | custom-call | flops 2181038080 | bytes 1048576 | tf_op jit(solution)/shard_map/pallas_call | solution.py:464
  37.4 0.7 %shard_map.112 = (f32[64,256]{1,0:T(8,128)}, f32[64,256]{1,0:T(8,128)}, f32[64,256]{1,0:T(8,128)}, f32[32,64]{1,0:T(8,128)}) custom-call(f32[64,256]{1,0:T(8,128)S(1)} %get-tuple-element.12.refs_0_, f32[64,256]{1,0:T(8,128)S(1)} %get-tuple-element.13.refs_1_, f32[64,256]{1,0:T(8,128)S(1)} %get-tuple-element.14.refs_2_, f32[32,64]{1,0:T(8,128)S(1)} %get-tuple-element.15.refs_3_), custom_call_target="tpu_custom_call" | custom-call | tf_op jit(solution)/shard_map/pallas_call | solution.py:516

commit v6 on v5

--- a/solution.py
+++ b/solution.py
@@ -74,7 +74,7 @@
     est_ref, res_ref, dir_ref, ker_ref, w_ref, fin_ref, bias_ref, fout_ref, fetch_s,
     edge, edge_halo, kscr, kt, ktj, facc, shaped, hb, hz, ishift, acc,
     part, rsbuf, iblk, iwin, part2, rsbuf2, sca, sca_in, ag, scb, ext,
-    h_s, h_r, rs_s, rs_r, iw_s, in_s, iw_r, rt_s, rt_r, sa_s, sa_r, ag_s, ag_r, sb_s, sb_r,
+    h_s, h_r, rs_s, rs_r, iw_s, iw_r, rt_s, rt_r, sa_s, sa_r, ag_s, ag_r, sb_s, sb_r,
 ):
     ci = lax.axis_index("comp")
     bi = lax.axis_index("band")
@@ -83,11 +83,9 @@
     comps = w_ref.shape[0]
     half_nc = nc // 2
 
-    def peers(fn):
-        loop(1, nc, lambda d: fn(lax.rem(ci + d, nc)))
-
-    def bands(fn):
-        loop(1, nb, lambda d: fn(lax.rem(bi + d, nb)))
+    def whole(ref, count, send, recv):
+        slots = ref.at[pl.ds(0, count)]
+        return remote(slots, slots, send.at[0], recv.at[0], ci, up)
 
     def ring(d, n):
         return min(d, n - d)
@@ -130,12 +128,13 @@
     def greet(comp, band):
         pl.semaphore_signal(barrier, inc=1, device_id=(comp, band), device_id_type=MESH)
 
-    def greet_both(c):
+    for c in range(nc):
         greet(c, up)
         greet(c, down)
-    loop(0, nc, greet_both)
-    peers(lambda j: greet(j, bi))
-    loop(2, nb - 1, lambda d: greet(ci, lax.rem(bi + d, nb)))
+    for hops, j in far_peers:
+        greet(j, bi)
+    for d in range(2, nb - 1):
+        greet(ci, lax.rem(bi + d, nb))
 
     kscr[...] = jnp.zeros_like(kscr)
     fetches[0].wait()
@@ -207,22 +206,18 @@
     pl.semaphore_wait(barrier, nc - 1 + 2 * nc + nb - 3)
 
     def rs_up(c):
-        return remote(part.at[c], rsbuf.at[nc + ci], rs_s.at[c], rs_r.at[nc + ci], c + half_nc, up)
+        return remote(part.at[c], rsbuf.at[nc + ci], rs_s.at[0], rs_r.at[0], c + half_nc, up)
 
     def rs_down(c):
         return remote(
-            part.at[12 + c], rsbuf.at[nc + ci], rs_s.at[12 + c], rs_r.at[nc + ci], c, down)
+            part.at[12 + c], rsbuf.at[nc + ci], rs_s.at[0], rs_r.at[0], c, down)
 
     def rs(j):
-        return remote(part.at[4 + j], rsbuf.at[ci], rs_s.at[4 + j], rs_r.at[ci], j, bi)
-
-    def rs_in(slot):
-        return remote(part.at[0], rsbuf.at[slot], rs_s.at[0], rs_r.at[slot], ci, up)
-
-    def start_far(c):
+        return remote(part.at[4 + j], rsbuf.at[ci], rs_s.at[0], rs_r.at[0], j, bi)
+
+    for c in range(half_nc):
         rs_up(c).start()
         rs_down(c).start()
-    loop(0, half_nc, start_far)
     far_first(to_peers(lambda j: rs(j).start()))
     edges = [
         remote(edge.at[0], edge_halo.at[1], h_s.at[0], h_r.at[1], ci, up),
@@ -231,11 +226,8 @@
     for copy in edges:
         copy.start()
 
-    def end_far(c):
-        rs_up(c).wait_send()
-        rs_down(c).wait_send()
-    ends.append(lambda: loop(0, half_nc, end_far))
-    ends.append(lambda: peers(lambda j: rs(j).wait_send()))
+    scattered = whole(part, 2 * nc - 1, rs_s, rs_r)
+    ends.append(scattered.wait_send)
     ends.extend(copy.wait_send for copy in edges)
 
     size = 128
@@ -257,8 +249,7 @@
         hz[k] = band_matrix(ktj, k, HALF).astype(BF16)
 
     rsbuf[ci] = part[4 + ci]
-    peers(lambda j: rs_in(j).wait_recv())
-    loop(0, nc, lambda j: rs_in(nc + j).wait_recv())
+    scattered.wait_recv()
     far = lax.div(ci, half_nc)
     near = rsbuf[0]
     away = rsbuf[nc]
@@ -273,23 +264,16 @@
     far_slot = ci + 12 - 16 * far
 
     def to_peer(j):
-        return remote(iblk, iwin.at[ci + 4], iw_s.at[j], iw_r.at[ci + 4], j, bi)
+        return remote(iblk, iwin.at[ci + 4], iw_s.at[0], iw_r.at[0], j, bi)
 
     def to_far(j):
-        return remote(iblk, iwin.at[far_slot], in_s.at[j], iw_r.at[far_slot], j, far_band)
-    loop(0, nc, lambda j: to_far(j).start())
+        return remote(iblk, iwin.at[far_slot], iw_s.at[0], iw_r.at[0], j, far_band)
+    for j in range(nc):
+        to_far(j).start()
     far_first(to_peers(lambda j: to_peer(j).start()))
-    ends.append(lambda: peers(lambda j: to_peer(j).wait_send()))
-    ends.append(lambda: loop(0, nc, lambda j: to_far(j).wait_send()))
-
-    def window(at):
-        return remote(iblk, iwin.at[at], iw_s.at[0], iw_r.at[at], ci, up)
-    peers(lambda j: window(j + 4).wait_recv())
-
-    def wait_far(j):
-        window(j).wait_recv()
-        window(j + 12).wait_recv()
-    loop(0, 4, wait_far)
+    shown = whole(iwin, 2 * nc - 1, iw_s, iw_r)
+    ends.append(shown.wait_send)
+    shown.wait_recv()
 
     inside = ((bi > 0).astype(F32), (bi < nb - 1).astype(F32))
     for r in range(0, 16, 2):
@@ -317,22 +301,24 @@
         part2[j] = rsum[8 * j:8 * j + 8]
 
     def rt(j, slot):
-        return remote(part2.at[j], rsbuf2.at[slot], rt_s.at[j], rt_r.at[slot], j, bi)
-    ends.append(lambda: peers(lambda j: rt(j, ci).wait_send()))
+        return remote(part2.at[j], rsbuf2.at[slot], rt_s.at[0], rt_r.at[0], j, bi)
+    reduced = whole(rsbuf2, nc - 1, rt_s, rt_r)
+    ends.append(reduced.wait_send)
     sca[0:1] = fold(dir_ref[...] * rsum)
 
     def sa(b, slot):
-        return remote(sca, sca_in.at[slot], sa_s.at[b], sa_r.at[slot], ci, b)
+        return remote(sca, sca_in.at[slot], sa_s.at[0], sa_r.at[0], ci, b)
     far_first(to_peers(lambda j: rt(j, ci).start()) + to_bands(lambda b: sa(b, bi).start()))
-    ends.append(lambda: bands(lambda b: sa(b, bi).wait_send()))
+    products = whole(sca_in, nb - 1, sa_s, sa_r)
+    ends.append(products.wait_send)
     sca_in[bi] = sca[...]
     rsbuf2[ci] = part2[ci]
 
-    peers(lambda j: rt(j, j).wait_recv())
+    reduced.wait_recv()
     block = rsbuf2[0]
     for j in range(1, nc):
         block += rsbuf2[j]
-    bands(lambda b: sa(b, b).wait_recv())
+    products.wait_recv()
     scalars = sca_in[0]
     for b in range(1, nb):
         scalars += sca_in[b]
@@ -341,10 +327,11 @@
     ag[ci, 2] = scalars
 
     def gather(j, slot):
-        return remote(ag.at[ci], ag.at[slot], ag_s.at[j], ag_r.at[slot], j, bi)
+        return remote(ag.at[ci], ag.at[slot], ag_s.at[0], ag_r.at[0], j, bi)
     far_first(to_peers(lambda j: gather(j, ci).start()))
-    ends.append(lambda: peers(lambda j: gather(j, ci).wait_send()))
-    peers(lambda j: gather(j, j).wait_recv())
+    gathered = whole(ag, nc - 1, ag_s, ag_r)
+    ends.append(gathered.wait_send)
+    gathered.wait_recv()
 
     product = ag[0, 2, 0:1]
     for j in range(1, nc):
@@ -361,9 +348,10 @@
     scb[nb] = jnp.broadcast_to(fold(updated * updated), (8, 128))
 
     def sb(b, slot):
-        return remote(scb.at[nb], scb.at[slot], sb_s.at[b], sb_r.at[slot], ci, b)
+        return remote(scb.at[nb], scb.at[slot], sb_s.at[0], sb_r.at[0], ci, b)
     far_first(to_bands(lambda b: sb(b, bi).start()))
-    ends.append(lambda: bands(lambda b: sb(b, bi).wait_send()))
+    squares = whole(scb, nb - 1, sb_s, sb_r)
+    ends.append(squares.wait_send)
     scb[bi] = scb[nb]
     for copy in edges:
         copy.wait_recv()
@@ -428,15 +416,14 @@
     centre = pltpu.roll(tile[2:2 + ROWS], 126, 1)
     den_ref[...] = (centre - mixed).T[:columns]
 
-    bands(lambda b: sb(b, b).wait_recv())
+    for end in ends:
+        end()
+    squares.wait_recv()
     new = scb[0, 0:1]
     for b in range(1, nb):
         new += scb[b, 0:1]
     new = jnp.sum(new, axis=1, keepdims=True)
     dn_ref[...] = rn_ref[...] + (new / old) * dir_ref[...]
-
-    for end in ends:
-        end()
 
 
 def place(*refs):
@@ -499,12 +486,7 @@
             pltpu.VMEM((nb + 1, 8, 128), F32),
             pltpu.VMEM((80, WIDTH), F32),
             dma((2,)), dma((2,)),
-            dma((16,)), dma((2 * nc,)),
-            dma((nc,)), dma((nc,)), dma((16,)),
-            dma((nc,)), dma((nc,)),
-            dma((nb,)), dma((nb,)),
-            dma((nc,)), dma((nc,)),
-            dma((nb,)), dma((nb,)),
+            *([dma((1,))] * 12),
         ],
         compiler_params=pltpu.CompilerParams(
             collective_id=0, has_side_effects=True, vmem_limit_bytes=48 * 1024 * 1024),

time: 38.3 us -> 35.7 us (0.932)
  Pallas kernels: 37.4 us -> 35 us
    pallas_call x1, Pallas kernels: 36.7 us -> 34.3 us  [per_device(): pl.pallas_call(functools.partial(kernel, nc, nb, unroll), out_shape=shape...]
where the time goes in v6:
time: 35.7 us; the launch traced here: 35.6 us
  Pallas kernels  35 us (98%)
  between operations  0.64 us (2%)
    pallas_call x1, Pallas kernels, per_device(): pl.pallas_call(functools.partial(kernel, nc, nb, unroll), out_shape=shape...  34.3 us

profile of v6, /device:TPU:1, one launch (start us, length us, event | category | flops | bytes accessed | tf_op | source)
XLA Modules:
  0.0 35.6 jit_solution(10184564890348196452)
XLA Ops:
  0.6 34.3 %shard_map.111 = (f32[64,256]{1,0:T(8,128)S(1)}, f32[64,256]{1,0:T(8,128)S(1)}, f32[64,256]{1,0:T(8,128)S(1)}, f32[32,64]{1,0:T(8,128)S(1)}) custom-call(f32[64,256]{1,0:T(8,128)} %est_hbm.1, f32[64,256]{1,0:T(8,128)} %res_hbm.1, f32[64,256]{1,0:T(8,128)} %dir_hbm.1, bf16[65,4,65]{2,1,0:T(4,128)(2,1)} %bitcast.4, bf16[4,64,256]{2,1,0:T(8,128)(2,1)} %w_hbm.1, ...), custom_call_target="tpu_custom_call" | custom-call | flops 2181038080 | bytes 1048576 | tf_op jit(solution)/shard_map/pallas_call | solution.py:451
  34.9 0.7 %shard_map.112 = (f32[64,256]{1,0:T(8,128)}, f32[64,256]{1,0:T(8,128)}, f32[64,256]{1,0:T(8,128)}, f32[32,64]{1,0:T(8,128)}) custom-call(f32[64,256]{1,0:T(8,128)S(1)} %get-tuple-element.12.refs_0_, f32[64,256]{1,0:T(8,128)S(1)} %get-tuple-element.13.refs_1_, f32[64,256]{1,0:T(8,128)S(1)} %get-tuple-element.14.refs_2_, f32[32,64]{1,0:T(8,128)S(1)} %get-tuple-element.15.refs_3_), custom_call_target="tpu_custom_call" | custom-call | tf_op jit(solution)/shard_map/pallas_call | solution.py:498

commit v7 on v6

--- a/solution.py
+++ b/solution.py
@@ -200,9 +200,7 @@
     edge[1, 0] = est_ref[ROWS - 8:]
     edge[1, 1] = dir_ref[ROWS - 8:]
     residual = res_ref[...]
-    sca[...] = jnp.zeros_like(sca)
-    sca[1:2] = fold(direction * direction)
-    sca[2:3] = fold(residual * residual)
+    energies = (fold(direction * direction), fold(residual * residual))
     pl.semaphore_wait(barrier, nc - 1 + 2 * nc + nb - 3)
 
     def rs_up(c):
@@ -289,13 +287,15 @@
             ishift[at, pl.ds(8 * r, 16), :] = value
 
     rsum = jnp.zeros((ROWS, WIDTH), F32)
+    for side in range(2):
+        for k in range(comps):
+            source = ishift[pl.ds(1 + side * BACK_FINE, BACK_FINE)].reshape(BACK_FINE * 128, WIDTH)
+            acc[k, side] = jnp.dot(hb[side, k], source, preferred_element_type=F32)
     for k in range(comps):
         back = jnp.dot(hz[k], ishift[0], preferred_element_type=F32)
         for side, sign in ((0, 1), (1, -1)):
-            source = ishift[pl.ds(1 + side * BACK_FINE, BACK_FINE)].reshape(BACK_FINE * 128, WIDTH)
-            acc[...] = jnp.dot(hb[side, k], source, preferred_element_type=F32)
             for s1 in range(BACK_COARSE):
-                back += lane_shift(acc[pl.ds(s1 * ROWS, ROWS), :], sign * BACK_FINE * s1)
+                back += lane_shift(acc[k, side, pl.ds(s1 * ROWS, ROWS), :], sign * BACK_FINE * s1)
         rsum += w_ref[k].astype(F32) * back
     for j in range(8):
         part2[j] = rsum[8 * j:8 * j + 8]
@@ -304,7 +304,13 @@
         return remote(part2.at[j], rsbuf2.at[slot], rt_s.at[0], rt_r.at[0], j, bi)
     reduced = whole(rsbuf2, nc - 1, rt_s, rt_r)
     ends.append(reduced.wait_send)
-    sca[0:1] = fold(dir_ref[...] * rsum)
+    lane_row = lax.broadcasted_iota(jnp.int32, (1, 128), 1)
+    quarters = []
+    for x in (fold(dir_ref[...] * rsum), *energies):
+        x = x + pltpu.roll(x, 64, 1)
+        quarters.append(x + pltpu.roll(x, 32, 1))
+    sca[...] = jnp.where(
+        lane_row < 32, quarters[0], jnp.where(lane_row < 64, quarters[1], quarters[2]))
 
     def sa(b, slot):
         return remote(sca, sca_in.at[slot], sa_s.at[0], sa_r.at[0], ci, b)
@@ -324,7 +330,7 @@
         scalars += sca_in[b]
     ag[ci, 0] = block[:, :128]
     ag[ci, 1] = block[:, 128:]
-    ag[ci, 2] = scalars
+    ag[ci, 2] = jnp.broadcast_to(scalars, (8, 128))
 
     def gather(j, slot):
         return remote(ag.at[ci], ag.at[slot], ag_s.at[0], ag_r.at[0], j, bi)
@@ -336,8 +342,10 @@
     product = ag[0, 2, 0:1]
     for j in range(1, nc):
         product += ag[j, 2, 0:1]
-    product = product + DAMPING * ag[0, 2, 1:2]
-    old = jnp.sum(ag[0, 2, 2:3], axis=1, keepdims=True)
+    scalars = ag[0, 2, 0:1]
+    product = jnp.where(lane_row < 32, product, jnp.where(lane_row < 64, DAMPING * scalars, 0.0))
+    squared = jnp.where((lane_row >= 64) & (lane_row < 96), scalars, 0.0)
+    old = jnp.sum(squared, axis=1, keepdims=True)
     alpha = old / jnp.sum(product, axis=1, keepdims=True)
 
     for j in range(8):
@@ -345,7 +353,7 @@
             at = (slice(8 * j, 8 * j + 8), slice(128 * c, 128 * c + 128))
             rn_ref[at] = res_ref[at] - alpha * (ag[j, c] + DAMPING * dir_ref[at])
     updated = rn_ref[...]
-    scb[nb] = jnp.broadcast_to(fold(updated * updated), (8, 128))
+    scb[nb] = fold(updated * updated)
 
     def sb(b, slot):
         return remote(scb.at[nb], scb.at[slot], sb_s.at[0], sb_r.at[0], ci, b)
@@ -419,9 +427,9 @@
     for end in ends:
         end()
     squares.wait_recv()
-    new = scb[0, 0:1]
+    new = scb[0]
     for b in range(1, nb):
-        new += scb[b, 0:1]
+        new += scb[b]
     new = jnp.sum(new, axis=1, keepdims=True)
     dn_ref[...] = rn_ref[...] + (new / old) * dir_ref[...]
 
@@ -473,17 +481,17 @@
             pltpu.VMEM((2, comps, BACK_COARSE * ROWS, BACK_FINE * 128), BF16),
             pltpu.VMEM((comps, ROWS, 128), BF16),
             pltpu.VMEM((1 + 2 * BACK_FINE, 128, WIDTH), BF16),
-            pltpu.VMEM((BACK_COARSE * ROWS, WIDTH), F32),
+            pltpu.VMEM((comps, 2, BACK_COARSE * ROWS, WIDTH), F32),
             pltpu.VMEM((16, 8, WIDTH), F32),
             pltpu.VMEM((2 * nc, 8, WIDTH), F32),
             pltpu.VMEM((16, 128), BF16),
             pltpu.VMEM((16, 16, 128), BF16),
             pltpu.VMEM((8, 8, WIDTH), F32),
             pltpu.VMEM((8, 8, WIDTH), F32),
-            pltpu.VMEM((8, 128), F32),
-            pltpu.VMEM((nb, 8, 128), F32),
+            pltpu.VMEM((1, 128), F32),
+            pltpu.VMEM((nb, 1, 128), F32),
             pltpu.VMEM((nc, 3, 8, 128), F32),
-            pltpu.VMEM((nb + 1, 8, 128), F32),
+            pltpu.VMEM((nb + 1, 1, 128), F32),
             pltpu.VMEM((80, WIDTH), F32),
             dma((2,)), dma((2,)),
             *([dma((1,))] * 12),

time: 35.7 us -> 35.8 us (level)
  no operation moved by 1% of the time
where the time goes in v7:
time: 35.8 us; the launch traced here: 35.6 us
  Pallas kernels  35 us (98%)
  between operations  0.64 us (2%)
    pallas_call x1, Pallas kernels, per_device(): pl.pallas_call(functools.partial(kernel, nc, nb, unroll), out_shape=shape...  34.3 us

profile of v7, /device:TPU:1, one launch (start us, length us, event | category | flops | bytes accessed | tf_op | source)
XLA Modules:
  0.0 35.6 jit_solution(6627732733324125708)
XLA Ops:
  0.6 34.3 %shard_map.111 = (f32[64,256]{1,0:T(8,128)S(1)}, f32[64,256]{1,0:T(8,128)S(1)}, f32[64,256]{1,0:T(8,128)S(1)}, f32[32,64]{1,0:T(8,128)S(1)}) custom-call(f32[64,256]{1,0:T(8,128)} %est_hbm.1, f32[64,256]{1,0:T(8,128)} %res_hbm.1, f32[64,256]{1,0:T(8,128)} %dir_hbm.1, bf16[65,4,65]{2,1,0:T(4,128)(2,1)} %bitcast.4, bf16[4,64,256]{2,1,0:T(8,128)(2,1)} %w_hbm.1, ...), custom_call_target="tpu_custom_call" | custom-call | flops 2181038080 | bytes 1048576 | tf_op jit(solution)/shard_map/pallas_call | solution.py:459
  34.9 0.7 %shard_map.112 = (f32[64,256]{1,0:T(8,128)}, f32[64,256]{1,0:T(8,128)}, f32[64,256]{1,0:T(8,128)}, f32[32,64]{1,0:T(8,128)}) custom-call(f32[64,256]{1,0:T(8,128)S(1)} %get-tuple-element.12.refs_0_, f32[64,256]{1,0:T(8,128)S(1)} %get-tuple-element.13.refs_1_, f32[64,256]{1,0:T(8,128)S(1)} %get-tuple-element.14.refs_2_, f32[32,64]{1,0:T(8,128)S(1)} %get-tuple-element.15.refs_3_), custom_call_target="tpu_custom_call" | custom-call | tf_op jit(solution)/shard_map/pallas_call | solution.py:506

commit v8 on v7

--- a/solution.py
+++ b/solution.py
@@ -74,7 +74,7 @@
     est_ref, res_ref, dir_ref, ker_ref, w_ref, fin_ref, bias_ref, fout_ref, fetch_s,
     edge, edge_halo, kscr, kt, ktj, facc, shaped, hb, hz, ishift, acc,
     part, rsbuf, iblk, iwin, part2, rsbuf2, sca, sca_in, ag, scb, ext,
-    h_s, h_r, rs_s, rs_r, iw_s, iw_r, rt_s, rt_r, sa_s, sa_r, ag_s, ag_r, sb_s, sb_r,
+    h_s, h_r, rs_s, rs_r, iw_s, iw_r, in_r, rt_s, rt_r, sa_s, sa_r, ag_s, ag_r, sb_s, sb_r,
 ):
     ci = lax.axis_index("comp")
     bi = lax.axis_index("band")
@@ -265,16 +265,20 @@
         return remote(iblk, iwin.at[ci + 4], iw_s.at[0], iw_r.at[0], j, bi)
 
     def to_far(j):
-        return remote(iblk, iwin.at[far_slot], iw_s.at[0], iw_r.at[0], j, far_band)
+        return remote(iblk, iwin.at[far_slot], iw_s.at[0], in_r.at[0], j, far_band)
     for j in range(nc):
         to_far(j).start()
     far_first(to_peers(lambda j: to_peer(j).start()))
     shown = whole(iwin, 2 * nc - 1, iw_s, iw_r)
     ends.append(shown.wait_send)
-    shown.wait_recv()
+    near_rows = whole(iwin, nc - 1, iw_s, iw_r)
+    far_rows = whole(iwin, nc, iw_s, in_r)
+    near_rows.wait_recv()
 
     inside = ((bi > 0).astype(F32), (bi < nb - 1).astype(F32))
-    for r in range(0, 16, 2):
+    for r in (4, 6, 8, 10, 0, 2, 12, 14):
+        if r == 0:
+            far_rows.wait_recv()
         first, second = iwin[r].astype(F32), iwin[r + 1].astype(F32)
         pair = jnp.concatenate([
             jnp.concatenate([first[:8], first[8:]], axis=1),
@@ -494,7 +498,7 @@
             pltpu.VMEM((nb + 1, 1, 128), F32),
             pltpu.VMEM((80, WIDTH), F32),
             dma((2,)), dma((2,)),
-            *([dma((1,))] * 12),
+            *([dma((1,))] * 13),
         ],
         compiler_params=pltpu.CompilerParams(
             collective_id=0, has_side_effects=True, vmem_limit_bytes=48 * 1024 * 1024),

time: 35.8 us -> 36 us (level)
  no operation moved by 1% of the time
where the time goes in v8:
time: 36 us; the launch traced here: 35.8 us
  Pallas kernels  35.2 us (98%)
  between operations  0.64 us (2%)
    pallas_call x1, Pallas kernels, per_device(): pl.pallas_call(functools.partial(kernel, nc, nb, unroll), out_shape=shape...  34.5 us

profile of v8, /device:TPU:1, one launch (start us, length us, event | category | flops | bytes accessed | tf_op | source)
XLA Modules:
  0.0 35.8 jit_solution(16505882386015885022)
XLA Ops:
  0.6 34.5 %shard_map.111 = (f32[64,256]{1,0:T(8,128)S(1)}, f32[64,256]{1,0:T(8,128)S(1)}, f32[64,256]{1,0:T(8,128)S(1)}, f32[32,64]{1,0:T(8,128)S(1)}) custom-call(f32[64,256]{1,0:T(8,128)} %est_hbm.1, f32[64,256]{1,0:T(8,128)} %res_hbm.1, f32[64,256]{1,0:T(8,128)} %dir_hbm.1, bf16[65,4,65]{2,1,0:T(4,128)(2,1)} %bitcast.4, bf16[4,64,256]{2,1,0:T(8,128)(2,1)} %w_hbm.1, ...), custom_call_target="tpu_custom_call" | custom-call | flops 2181038080 | bytes 1048576 | tf_op jit(solution)/shard_map/pallas_call | solution.py:463
  35.1 0.7 %shard_map.112 = (f32[64,256]{1,0:T(8,128)}, f32[64,256]{1,0:T(8,128)}, f32[64,256]{1,0:T(8,128)}, f32[32,64]{1,0:T(8,128)}) custom-call(f32[64,256]{1,0:T(8,128)S(1)} %get-tuple-element.12.refs_0_, f32[64,256]{1,0:T(8,128)S(1)} %get-tuple-element.13.refs_1_, f32[64,256]{1,0:T(8,128)S(1)} %get-tuple-element.14.refs_2_, f32[32,64]{1,0:T(8,128)S(1)} %get-tuple-element.15.refs_3_), custom_call_target="tpu_custom_call" | custom-call | tf_op jit(solution)/shard_map/pallas_call | solution.py:510

commit v9 on v7

--- a/solution.py
+++ b/solution.py
@@ -128,11 +128,11 @@
     def greet(comp, band):
         pl.semaphore_signal(barrier, inc=1, device_id=(comp, band), device_id_type=MESH)
 
-    for c in range(nc):
-        greet(c, up)
-        greet(c, down)
-    for hops, j in far_peers:
-        greet(j, bi)
+    over = [
+        (hops + 1, lambda j=j, b=b: greet(j, b))
+        for hops, j in far_peers + [(0, ci)] for b in (up, down)
+    ]
+    far_first(over + to_peers(lambda j: greet(j, bi)))
     for d in range(2, nb - 1):
         greet(ci, lax.rem(bi + d, nb))
 
@@ -266,9 +266,8 @@
 
     def to_far(j):
         return remote(iblk, iwin.at[far_slot], iw_s.at[0], iw_r.at[0], j, far_band)
-    for j in range(nc):
-        to_far(j).start()
-    far_first(to_peers(lambda j: to_peer(j).start()))
+    over = [(hops + 1, lambda j=j: to_far(j).start()) for hops, j in far_peers + [(0, ci)]]
+    far_first(over + to_peers(lambda j: to_peer(j).start()))
     shown = whole(iwin, 2 * nc - 1, iw_s, iw_r)
     ends.append(shown.wait_send)
     shown.wait_recv()

time: 35.8 us -> 35.7 us (level)
  no operation moved by 1% of the time
where the time goes in v9:
time: 35.7 us; the launch traced here: 35.3 us
  Pallas kernels  34.7 us (97%)
  between operations  0.64 us (2%)
    pallas_call x1, Pallas kernels, per_device(): pl.pallas_call(functools.partial(kernel, nc, nb, unroll), out_shape=shape...  34 us

profile of v9, /device:TPU:1, one launch (start us, length us, event | category | flops | bytes accessed | tf_op | source)
XLA Modules:
  0.0 35.3 jit_solution(18166414636476251187)
XLA Ops:
  0.6 34.0 %shard_map.111 = (f32[64,256]{1,0:T(8,128)S(1)}, f32[64,256]{1,0:T(8,128)S(1)}, f32[64,256]{1,0:T(8,128)S(1)}, f32[32,64]{1,0:T(8,128)S(1)}) custom-call(f32[64,256]{1,0:T(8,128)} %est_hbm.1, f32[64,256]{1,0:T(8,128)} %res_hbm.1, f32[64,256]{1,0:T(8,128)} %dir_hbm.1, bf16[65,4,65]{2,1,0:T(4,128)(2,1)} %bitcast.4, bf16[4,64,256]{2,1,0:T(8,128)(2,1)} %w_hbm.1, ...), custom_call_target="tpu_custom_call" | custom-call | flops 2181038080 | bytes 1048576 | tf_op jit(solution)/shard_map/pallas_call | solution.py:458
  34.6 0.7 %shard_map.112 = (f32[64,256]{1,0:T(8,128)}, f32[64,256]{1,0:T(8,128)}, f32[64,256]{1,0:T(8,128)}, f32[32,64]{1,0:T(8,128)}) custom-call(f32[64,256]{1,0:T(8,128)S(1)} %get-tuple-element.12.refs_0_, f32[64,256]{1,0:T(8,128)S(1)} %get-tuple-element.13.refs_1_, f32[64,256]{1,0:T(8,128)S(1)} %get-tuple-element.14.refs_2_, f32[32,64]{1,0:T(8,128)S(1)} %get-tuple-element.15.refs_3_), custom_call_target="tpu_custom_call" | custom-call | tf_op jit(solution)/shard_map/pallas_call | solution.py:505
